TPU v7x, 512 devices: a whole 4x8x8 slice. The times are simulated.
512 devices in a mesh: dp: 8 (over z), expert: 64 (over x, y, core).
Axes of the slice: x: 4, y: 8, z: 8, core: 2. Of those that a mesh axis runs over, the one named last changes fastest.
Arguments:
- query_nope: bfloat16 [2048, 128, 128], P(('dp', 'expert')), may hold values from -6 to 6
- query_rope: bfloat16 [2048, 128, 64], P(('dp', 'expert')), may hold values from -320 to 320
- latent_cache: bfloat16 [2048, 512, 512], P(('dp', 'expert')), may hold values from -6 to 6
- key_rope: bfloat16 [2048, 512, 64], P(('dp', 'expert')), may hold values from -4 to 4
- lengths: int32 [2048], P(('dp', 'expert')), may hold values from 64 to 512, as said below
- key_weight: bfloat16 [128, 128, 512], P('expert', 'dp'), may hold values from -0.5 to 0.5
- expert_input: bfloat16 [2048, 7168], P(('dp', 'expert')), may hold values from -6 to 6
- route_slots: int32 [2048, 2], P(('dp', 'expert')), may hold values from 0 to 7, all different within a row; in each aligned block of 4 rows (0 to 3, 4 to 7, ...) at most 2 rows name the same one
- route_gates: float32 [2048, 2], P(('dp', 'expert')), may hold values from 0.1 to 1
- trainer_gate_up: bfloat16 [8, 2048, 2, 7168], P(None, 'expert', None, 'dp'), may hold values from -0.0625 to 0.0625
- trainer_down: bfloat16 [8, 2048, 7168], P(None, 'expert', 'dp'), may hold values from -0.125 to 0.125
- trainer_order: int32 [8], replicated, may hold values from 0 to 7, each once
- rollout_order: int32 [8], replicated, may hold values from 0 to 7, each once
Outputs:
- latent_output: bfloat16 [2048, 128, 512], P(('dp', 'expert'))
- expert_output: bfloat16 [2048, 7168], P(('dp', 'expert'))
Inputs may be any that keep to these rules, and one draw needn't show every extreme that they name: `route_slots`: each row names 2 different slots. Within the rows of one device (aligned blocks of 4 rows) no slot is named by more than 2 rows, and in some block a slot is named by exactly 2 rows. A permutation: trainer position i holds expert trainer_order[i]. A permutation: rollout slot g holds expert rollout_order[g]. `lengths`: among the rows of one device some row has exactly 512 positions.
All inputs are finite; a program needn't handle non-finite values.
Results may differ from a plain program's by a relative error of at most 0.0069.
Values may be sent and summed in bfloat16 or wider, within the bound.
A program may use at most 128 MiB of HBM per device.

v0:
```python
import math

import jax
import jax.numpy as jnp
from jax import lax
from jax.sharding import PartitionSpec as P

NOPE = 128
ROPE = 64
CAP = 2


def regroup_select(selector, gate_up, down_rows, group_size):
    slab_size = gate_up.shape[0]
    share_size = gate_up.shape[1] // group_size
    gate_up = gate_up.reshape(slab_size, share_size, group_size, 2, gate_up.shape[3])
    down_rows = down_rows.reshape(slab_size, share_size, group_size, down_rows.shape[2])
    placed_gates = jnp.einsum(
        "gi,iksad->gskad", selector, gate_up, preferred_element_type=jnp.float32
    )
    placed_down = jnp.einsum(
        "gi,iksd->gskd", selector, down_rows, preferred_element_type=jnp.float32
    )
    total_devices = slab_size * group_size
    placed_gates = placed_gates.astype(jnp.bfloat16).reshape(
        total_devices, share_size, 2, placed_gates.shape[4]
    )
    placed_down = placed_down.astype(jnp.bfloat16).reshape(
        total_devices, share_size, placed_down.shape[3]
    )
    return (placed_gates, placed_down)


def on_device(
    query_nope,
    query_rope,
    latent_cache,
    key_rope,
    lengths,
    key_weight,
    expert_input,
    route_slots,
    route_gates,
    trainer_gate_up,
    trainer_down,
    trainer_order,
    rollout_order,
):
    expert_count = lax.axis_size("expert")
    local_rows, head_total, nope_width = query_nope.shape
    heads_here = head_total // expert_count
    slab_size = trainer_gate_up.shape[0]
    group_size = expert_count // slab_size
    selector = (trainer_order[None, :] == rollout_order[:, None]).astype(jnp.bfloat16)
    whole_gates, whole_down, key_full = (
        lax.all_gather(trainer_gate_up, "dp", axis=3, tiled=True),
        lax.all_gather(trainer_down, "dp", axis=2, tiled=True),
        lax.all_gather(key_weight, "dp", axis=1, tiled=True),
    )
    placed_gates, placed_down = regroup_select(selector, whole_gates, whole_down, group_size)
    gate_up_full, down_full = (
        lax.all_to_all(placed_gates, "expert", split_axis=0, concat_axis=0, tiled=True),
        lax.all_to_all(placed_down, "expert", split_axis=0, concat_axis=0, tiled=True),
    )
    slot_ids = jnp.arange(slab_size, dtype=jnp.int32)
    matches = route_slots[:, :, None] == slot_ids[None, None, :]
    routed = jnp.sum(matches.astype(jnp.int32), axis=1)
    gate_share = jnp.sum(
        jnp.where(matches, route_gates[:, :, None], jnp.zeros_like(route_gates)[:, :, None]), axis=1
    )
    before = jnp.cumsum(routed, axis=0) - routed
    places = jnp.arange(CAP, dtype=jnp.int32)
    placement = (routed[None, :, :] == 1) & (before[None, :, :] == places[:, None, None])
    placing = placement.astype(jnp.bfloat16)
    outgoing = jnp.einsum(
        "crg,rd->cgd", placing, expert_input, preferred_element_type=jnp.float32
    ).astype(jnp.bfloat16)
    model_width = outgoing.shape[2]
    outgoing = jnp.broadcast_to(
        outgoing[:, :, None, :], (CAP, slab_size, group_size, model_width)
    ).reshape(CAP, expert_count, model_width)
    query_send = query_nope.reshape(local_rows, expert_count, heads_here, nope_width)
    query_owned, tokens_owned = (
        lax.all_to_all(query_send, "expert", split_axis=1, concat_axis=0, tiled=True),
        lax.all_to_all(outgoing, "expert", split_axis=1, concat_axis=0, tiled=True),
    )
    query_owned = query_owned.reshape(expert_count * local_rows, heads_here, nope_width)
    rank_width = key_full.shape[2]
    query_latent = jnp.einsum(
        "rhn,hnk->rhk", query_owned, key_full, preferred_element_type=jnp.float32
    ).astype(jnp.bfloat16)
    returned = lax.all_to_all(
        query_latent.reshape(expert_count, local_rows, 1, heads_here, rank_width),
        "expert",
        split_axis=0,
        concat_axis=2,
        tiled=True,
    )
    query_latent = returned.reshape(local_rows, head_total, rank_width)
    score_scale = 1.0 / math.sqrt(NOPE + ROPE)
    scores = jnp.einsum(
        "rhk,rlk->rhl", query_latent, latent_cache, preferred_element_type=jnp.float32
    )
    scores = scores + jnp.einsum(
        "rhp,rlp->rhl", query_rope, key_rope, preferred_element_type=jnp.float32
    )
    scores = scores * score_scale
    visible = (
        jnp.arange(latent_cache.shape[1], dtype=jnp.int32)[None, None, :] < lengths[:, None, None]
    )
    scores = jnp.where(visible, scores, -jnp.inf)
    highest = jnp.max(scores, axis=2, keepdims=True)
    raised = jnp.exp(scores - highest)
    attention = (raised / jnp.sum(raised, axis=2, keepdims=True)).astype(jnp.bfloat16)
    latent_output = jnp.einsum(
        "rhl,rlk->rhk", attention, latent_cache, preferred_element_type=jnp.float32
    ).astype(jnp.bfloat16)
    tokens_owned = tokens_owned.reshape(expert_count * CAP, model_width)
    gate_up_full = gate_up_full.reshape(-1, 2, model_width)
    down_full = down_full.reshape(-1, model_width)
    projected = jnp.einsum(
        "rd,uad->aru", tokens_owned, gate_up_full, preferred_element_type=jnp.float32
    )
    hidden = (jax.nn.silu(projected[0]) * projected[1]).astype(jnp.bfloat16)
    partial_out = jnp.dot(hidden, down_full, preferred_element_type=jnp.float32).astype(
        jnp.bfloat16
    )
    coming_back = lax.all_to_all(
        partial_out.reshape(expert_count, CAP, model_width),
        "expert",
        split_axis=0,
        concat_axis=0,
        tiled=True,
    )
    summed = jnp.sum(
        coming_back.reshape(slab_size, group_size, CAP, model_width).astype(jnp.float32), axis=1
    )
    mixing = placement.astype(jnp.float32) * gate_share[None, :, :]
    expert_output = jnp.einsum(
        "crg,gcd->rd", mixing, summed, precision=lax.Precision.HIGHEST
    ).astype(jnp.bfloat16)
    return (latent_output, expert_output)


def solution(mesh):
    in_specs = (
        P(("dp", "expert"), None, None),
        P(("dp", "expert"), None, None),
        P(("dp", "expert"), None, None),
        P(("dp", "expert"), None, None),
        P(("dp", "expert")),
        P("expert", "dp", None),
        P(("dp", "expert"), None),
        P(("dp", "expert"), None),
        P(("dp", "expert"), None),
        P(None, "expert", None, "dp"),
        P(None, "expert", "dp"),
        P(),
        P(),
    )
    out_specs = (P(("dp", "expert"), None, None), P(("dp", "expert"), None))
    return jax.shard_map(
        on_device, mesh=mesh, in_specs=in_specs, out_specs=out_specs, check_vma=False
    )
```

profile of v0, /device:TPU:6, one launch (start us, length us, event | category | flops | bytes accessed | tf_op | source)
XLA Modules:
  0.0 474.1 jit_solution(7272527246261899094)
XLA Ops:
  8.7 1.7 copy.58
  10.3 10.8 %all-to-all-start = ((bf16[4,64,2,128]{3,0,2,1:T(4,128)(2,1)}), bf16[4,64,2,128]{3,0,2,1:T(4,128)(2,1)S(1)}, u32[]{:S(2)}, u32[]{:S(2)}) async-start(bf16[4,64,2,128]{3,0,2,1:T(4,128)(2,1)} %bitcast), calls=%async_computation | async-start | bytes 262144 | tf_op jit(solution)/shard_map/all_to_all | solution.py:84
  23.3 6.7 %all-to-all-done = bf16[4,64,2,128]{3,0,2,1:T(4,128)(2,1)S(1)} async-done(((bf16[4,64,2,128]{3,0,2,1:T(4,128)(2,1)}), bf16[4,64,2,128]{3,0,2,1:T(4,128)(2,1)S(1)}, u32[]{:S(2)}, u32[]{:S(2)}) %all-to-all-start) | async-done | bytes 131104 | tf_op jit(solution)/shard_map/all_to_all | solution.py:84
  30.0 2.2 broadcast_in_dim.34
  32.2 7.6 %all-to-all-start.3 = ((bf16[2,64,7168]{2,0,1:T(2,128)(2,1)}), bf16[2,64,7168]{2,0,1:T(2,128)(2,1)}, u32[]{:S(2)}, u32[]{:S(2)}) async-start(bf16[2,64,7168]{2,0,1:T(2,128)(2,1)} %bitcast.74), calls=%async_computation.3 | async-start | bytes 3670016 | tf_op jit(solution)/shard_map/all_to_all | solution.py:85
  39.8 28.2 %all-gather.5.cloned.1.call-done = bf16[8,32,7168]{2,1,0:T(8,128)(2,1)} async-done(((bf16[8,32,896]{2,1,0:T(8,128)(2,1)}), bf16[8,32,7168]{2,1,0:T(8,128)(2,1)}) %all-gather.5.cloned.1.call-update) | async-done | bytes 3670032 | tf_op jit(solution)/shard_map/all_gather | solution.py:57
  68.1 4.0 copy.67
  72.1 1.2 fusion.2
  73.3 2.0 copy.86
  75.3 4.8 %copy.69 = bf16[64,4,7168]{2,1,0:T(4,128)(2,1)} copy(bf16[64,4,7168]{2,0,1:T(8,128)(2,1)S(1)} %bitcast.72) | data formatting | bytes 7340032 | tf_op jit(solution)/shard_map/reshape | solution.py:28
  80.1 2.7 all-to-all-done.3
  82.8 8.6 %all-to-all-start.4 = ((bf16[64,4,7168]{2,1,0:T(4,128)(2,1)}), bf16[64,4,7168]{2,1,0:T(4,128)(2,1)}, u32[]{:S(2)}, u32[]{:S(2)}) async-start(bf16[64,4,7168]{2,1,0:T(4,128)(2,1)} %copy.69), calls=%async_computation.4 | async-start | bytes 7340032 | tf_op jit(solution)/shard_map/all_to_all | solution.py:63
  91.4 79.9 %all-gather.3.cloned.1.call-done = bf16[8,32,2,7168]{3,2,1,0:T(2,128)(2,1)} async-done(((bf16[8,32,2,896]{3,2,1,0:T(2,128)(2,1)}), bf16[8,32,2,7168]{3,2,1,0:T(2,128)(2,1)}) %all-gather.3.cloned.1.call-update) | async-done | bytes 7340048 | tf_op jit(solution)/shard_map/all_gather | solution.py:56
  171.3 9.1 %copy.62 = bf16[8,32,2,7168]{3,0,2,1:T(8,128)(2,1)S(1)} copy(bf16[8,32,2,7168]{3,2,1,0:T(2,128)(2,1)} %all-gather.3.cloned.1.call-done) | data formatting | bytes 14680064 | tf_op jit(solution)/shard_map/all_gather | solution.py:56
  180.5 5.1 %fusion.1 = bf16[8,8,4,2,7168]{4,0,3,1,2:T(8,128)(2,1)} fusion(bf16[8,4,8,2,7168]{4,0,3,2,1:T(8,128)(2,1)S(1)} %bitcast.71, s32[8]{0:T(128)S(1)} %copy-done.6, s32[8]{0:T(128)S(1)} %copy-done.7), kind=kOutput, calls=%fused_computation.2 | convolution fusion | flops 62390336 | bytes 14680128 | tf_op jit(solution)/shard_map/gi,iksad->gskad/dot_general | solution.py:18
  185.5 7.4 %copy.85 = bf16[8,8,4,2,7168]{4,1,0,3,2:T(8,128)(2,1)S(1)} copy(bf16[8,8,4,2,7168]{4,0,3,1,2:T(8,128)(2,1)} %fusion.1) | data formatting | bytes 14680064 | tf_op jit(solution)/shard_map/convert_element_type | solution.py:25
  192.9 22.5 %copy.64 = bf16[64,4,2,7168]{3,2,1,0:T(2,128)(2,1)} copy(bf16[64,4,2,7168]{3,0,2,1:T(8,128)(2,1)S(1)} %bitcast.70) | data formatting | bytes 14680064 | tf_op jit(solution)/shard_map/reshape | solution.py:25
  215.4 10.8 %all-to-all-start.2 = ((bf16[64,4,2,7168]{3,2,1,0:T(2,128)(2,1)}), bf16[64,4,2,7168]{3,2,1,0:T(2,128)(2,1)}, u32[]{:S(2)}, u32[]{:S(2)}) async-start(bf16[64,4,2,7168]{3,2,1,0:T(2,128)(2,1)} %copy.64), calls=%async_computation.2 | async-start | bytes 14680064 | tf_op jit(solution)/shard_map/all_to_all | solution.py:62
  226.2 24.9 %all_gather.9 = bf16[2,128,512]{2,1,0:T(8,128)(2,1)S(1)} all-gather(bf16[2,16,512]{2,1,0:T(8,128)(2,1)S(1)} %copy-done.4), channel_id=1, replica_groups=mesh['dp'=8,'expert'=64] {'dp'}, dimensions={1}, use_global_device_ids=true | all-gather | bytes 294912 | tf_op jit(solution)/shard_map/all_gather | solution.py:58
  252.6 4.9 %reshape.108 = bf16[128,7168,1]{1,0,2:T(8,128)(2,1)} reshape(bf16[64,2,1,7168]{3,1,0,2:T(2,128)(2,1)} %bitcast.17) | data formatting | bytes 3670016 | tf_op jit(solution)/shard_map/reshape | solution.py:118
  257.5 6.7 %reshape.103 = bf16[256,7168]{1,0:T(8,128)(2,1)} reshape(bf16[64,4,7168]{2,1,0:T(4,128)(2,1)} %all-to-all-done.4) | data formatting | bytes 7340032 | tf_op jit(solution)/shard_map/reshape | solution.py:120
  264.2 122.8 %all-to-all-done.2 = bf16[64,4,2,7168]{3,2,1,0:T(2,128)(2,1)} async-done(((bf16[64,4,2,7168]{3,2,1,0:T(2,128)(2,1)}), bf16[64,4,2,7168]{3,2,1,0:T(2,128)(2,1)}, u32[]{:S(2)}, u32[]{:S(2)}) %all-to-all-start.2) | async-done | bytes 7340064 | tf_op jit(solution)/shard_map/all_to_all | solution.py:62
  387.1 8.3 %all-to-all-start.1 = ((bf16[64,4,1,2,512]{4,1,3,2,0:T(4,128)(2,1)}), bf16[64,4,1,2,512]{4,1,3,2,0:T(4,128)(2,1)S(1)}, u32[]{:S(2)}, u32[]{:S(2)}) async-start(bf16[64,4,1,2,512]{4,1,3,2,0:T(4,128)(2,1)} %copy.60), calls=%async_computation.1 | async-start | bytes 1048576 | tf_op jit(solution)/shard_map/all_to_all | solution.py:92
  395.3 6.0 %fusion.11 = f32[2,128,256]{1,2,0:T(8,128)S(1)} fusion(bf16[128,7168,1]{1,0,2:T(8,128)(2,1)} %reshape.108, bf16[256,2,7168]{2,1,0:T(2,128)(2,1)} %bitcast.13), kind=kOutput, calls=%fused_computation.22 | convolution fusion | flops 939524096 | bytes 9437184 | tf_op jit(solution)/shard_map/rd,uad->aru/dot_general | solution.py:121
  401.4 1.9 convolution_convert_fusion.2
  403.3 4.8 %reshape.104 = bf16[64,2,7168]{2,1,0:T(2,128)(2,1)} reshape(bf16[128,7168]{1,0:T(8,128)(2,1)} %convolution_convert_fusion.2) | data formatting | bytes 3670016 | tf_op jit(solution)/shard_map/reshape | solution.py:129
  408.1 3.9 all-to-all-done.1
  412.0 7.5 %all-to-all-start.5 = ((bf16[64,2,7168]{2,1,0:T(2,128)(2,1)}), bf16[64,2,7168]{2,1,0:T(2,128)(2,1)}, u32[]{:S(2)}, u32[]{:S(2)}) async-start(bf16[64,2,7168]{2,1,0:T(2,128)(2,1)} %reshape.104), calls=%async_computation.5 | async-start | bytes 3670016 | tf_op jit(solution)/shard_map/all_to_all | solution.py:128
  421.2 1.9 convolution_convert_fusion.5
  423.1 39.5 %all-to-all-done.5 = bf16[64,2,7168]{2,1,0:T(2,128)(2,1)} async-done(((bf16[64,2,7168]{2,1,0:T(2,128)(2,1)}), bf16[64,2,7168]{2,1,0:T(2,128)(2,1)}, u32[]{:S(2)}, u32[]{:S(2)}) %all-to-all-start.5) | async-done | bytes 1835040 | tf_op jit(solution)/shard_map/all_to_all | solution.py:128
  462.6 3.3 convert_reduce_fusion
  465.9 1.1 fusion.3
  (40 shorter events, 6.7 us)
Async XLA Ops:
  7.2 412.6 %copy-start = (bf16[4,512,512]{2,1,0:T(8,128)(2,1)S(1)}, bf16[4,512,512]{2,1,0:T(8,128)(2,1)}, u32[]{:S(2)}) copy-start(bf16[4,512,512]{2,1,0:T(8,128)(2,1)} %param.15) | copy-start | bytes 6291460
  7.2 60.9 %all-gather.5.cloned.1.call-start = ((), (), s32[]{:S(2)}) async-start(), calls=%async_computation.7 | async-start | bytes 4128768 | tf_op jit(solution)/shard_map/all_gather | solution.py:57
  7.9 163.4 %all-gather.3.cloned.1.call-start = ((), (), s32[]{:S(2)}) async-start(), calls=%async_computation.6 | async-start | bytes 8257536 | tf_op jit(solution)/shard_map/all_gather | solution.py:56
  10.3 19.7 %all-to-all-start = ((bf16[4,64,2,128]{3,0,2,1:T(4,128)(2,1)}), bf16[4,64,2,128]{3,0,2,1:T(4,128)(2,1)S(1)}, u32[]{:S(2)}, u32[]{:S(2)}) async-start(bf16[4,64,2,128]{3,0,2,1:T(4,128)(2,1)} %bitcast), calls=%async_computation | async-start | bytes 262144 | tf_op jit(solution)/shard_map/all_to_all | solution.py:84
  32.2 50.6 %all-to-all-start.3 = ((bf16[2,64,7168]{2,0,1:T(2,128)(2,1)}), bf16[2,64,7168]{2,0,1:T(2,128)(2,1)}, u32[]{:S(2)}, u32[]{:S(2)}) async-start(bf16[2,64,7168]{2,0,1:T(2,128)(2,1)} %bitcast.74), calls=%async_computation.3 | async-start | bytes 3670016 | tf_op jit(solution)/shard_map/all_to_all | solution.py:85
  39.8 32.3 %copy-start.6 = (s32[8]{0:T(128)S(1)}, s32[8]{0:T(128)}, u32[]{:S(2)}) copy-start(s32[8]{0:T(128)} %param.24) | copy-start | bytes 100
  39.8 32.3 %copy-start.7 = (s32[8]{0:T(128)S(1)}, s32[8]{0:T(128)}, u32[]{:S(2)}) copy-start(s32[8]{0:T(128)} %param.25) | copy-start | bytes 100
  82.8 132.6 %all-to-all-start.4 = ((bf16[64,4,7168]{2,1,0:T(4,128)(2,1)}), bf16[64,4,7168]{2,1,0:T(4,128)(2,1)}, u32[]{:S(2)}, u32[]{:S(2)}) async-start(bf16[64,4,7168]{2,1,0:T(4,128)(2,1)} %copy.69), calls=%async_computation.4 | async-start | bytes 7340032 | tf_op jit(solution)/shard_map/all_to_all | solution.py:63
  215.4 10.8 %copy-start.4 = (bf16[2,16,512]{2,1,0:T(8,128)(2,1)S(1)}, bf16[2,16,512]{2,1,0:T(8,128)(2,1)}, u32[]{:S(2)}) copy-start(bf16[2,16,512]{2,1,0:T(8,128)(2,1)} %param.18) | copy-start | bytes 98308
  215.4 171.6 %all-to-all-start.2 = ((bf16[64,4,2,7168]{3,2,1,0:T(2,128)(2,1)}), bf16[64,4,2,7168]{3,2,1,0:T(2,128)(2,1)}, u32[]{:S(2)}, u32[]{:S(2)}) async-start(bf16[64,4,2,7168]{3,2,1,0:T(2,128)(2,1)} %copy.64), calls=%async_computation.2 | async-start | bytes 14680064 | tf_op jit(solution)/shard_map/all_to_all | solution.py:62
  387.1 25.0 %all-to-all-start.1 = ((bf16[64,4,1,2,512]{4,1,3,2,0:T(4,128)(2,1)}), bf16[64,4,1,2,512]{4,1,3,2,0:T(4,128)(2,1)S(1)}, u32[]{:S(2)}, u32[]{:S(2)}) async-start(bf16[64,4,1,2,512]{4,1,3,2,0:T(4,128)(2,1)} %copy.60), calls=%async_computation.1 | async-start | bytes 1048576 | tf_op jit(solution)/shard_map/all_to_all | solution.py:92
  395.3 6.0 %copy-start.1 = (bf16[256,7168]{1,0:T(8,128)(2,1)S(1)}, bf16[256,7168]{1,0:T(8,128)(2,1)}, u32[]{:S(2)}) copy-start(bf16[256,7168]{1,0:T(8,128)(2,1)} %reshape.103) | copy-start | bytes 11010052
  403.3 16.2 %copy-start.5 = (s32[4,2]{0,1:T(2,128)S(1)}, s32[4,2]{0,1:T(2,128)}, u32[]{:S(2)}) copy-start(s32[4,2]{0,1:T(2,128)} %param.20) | copy-start | bytes 100
  403.3 16.2 %copy-start.8 = (f32[4,2]{0,1:T(2,128)S(1)}, f32[4,2]{0,1:T(2,128)}, u32[]{:S(2)}) copy-start(f32[4,2]{0,1:T(2,128)} %param.21) | copy-start | bytes 100
  403.3 16.3 %copy-start.9 = (s32[4]{0:T(128)S(1)}, s32[4]{0:T(128)}, u32[]{:S(2)}) copy-start(s32[4]{0:T(128)} %param.17) | copy-start | bytes 52
  408.1 12.4 %copy-start.2 = (bf16[4,512,64]{1,2,0:T(8,128)(2,1)S(1)}, bf16[4,512,64]{1,2,0:T(8,128)(2,1)}, u32[]{:S(2)}) copy-start(bf16[4,512,64]{1,2,0:T(8,128)(2,1)} %param.16) | copy-start | bytes 786436
  408.1 12.4 %copy-start.3 = (bf16[4,128,64]{1,2,0:T(8,128)(2,1)S(1)}, bf16[4,128,64]{1,2,0:T(8,128)(2,1)}, u32[]{:S(2)}) copy-start(bf16[4,128,64]{1,2,0:T(8,128)(2,1)} %param.14) | copy-start | bytes 196612
  412.0 50.5 %all-to-all-start.5 = ((bf16[64,2,7168]{2,1,0:T(2,128)(2,1)}), bf16[64,2,7168]{2,1,0:T(2,128)(2,1)}, u32[]{:S(2)}, u32[]{:S(2)}) async-start(bf16[64,2,7168]{2,1,0:T(2,128)(2,1)} %reshape.104), calls=%async_computation.5 | async-start | bytes 3670016 | tf_op jit(solution)/shard_map/all_to_all | solution.py:128
Sparse Core Ops, SparseCore 0:
  10.1 57.9 all-gather.4
  70.1 101.2 all-gather.2
where the time goes:
time: 482 us; the launch traced here: 474 us
  waiting for transfers between devices  285 us (59%)
  local copies, waits for them, and re-layouts  71.6 us (15%)
  starting transfers between devices  53.5 us (11%)
  blocking collectives  24.9 us (5%)
  matrix products  19.7 us (4%)
  between operations  14.5 us (3%)
    all_to_all x1, waiting for transfers between devices, on_device(): lax.all_to_all(placed_gates, 'expert', split_axis=0, concat_axis=0, tiled...  123 us
    all_gather x1, waiting for transfers between devices, on_device(): lax.all_gather(trainer_gate_up, 'dp', axis=3, tiled=True)  79.9 us
    all_to_all x1, waiting for transfers between devices, on_device(): lax.all_to_all(partial_out.reshape(expert_count, CAP, model_width), 'expe...  39.5 us
    all_gather x1, waiting for transfers between devices, on_device(): lax.all_gather(trainer_down, 'dp', axis=2, tiled=True)  28.2 us
    all_gather x1, blocking collectives, on_device(): lax.all_gather(key_weight, 'dp', axis=1, tiled=True)  24.9 us
    reshape x1, local copies, waits for them, and re-layouts, regroup_select(): placed_gates.astype(jnp.bfloat16)  22.5 us
    all_to_all x1, starting transfers between devices, on_device(): lax.all_to_all(query_send, 'expert', split_axis=1, concat_axis=0, tiled=T...  10.8 us
    all_to_all x1, starting transfers between devices, on_device(): lax.all_to_all(placed_gates, 'expert', split_axis=0, concat_axis=0, tiled...  10.8 us
  transfers between devices with their start and end apart: 8, of which 7 were waited for; matrix products, arithmetic and copies ran while one was open for 19% of the time, Pallas kernels for 0%

commit v1 on v0

v1 whole, which is shorter than its diff:
```python
import math

import jax
import jax.numpy as jnp
import numpy as np
from jax import lax
from jax.experimental import pallas as pl
from jax.experimental.pallas import tpu as pltpu
from jax.sharding import PartitionSpec as P

NOPE = 128
ROPE = 64
NX, NY, NZ = 4, 8, 8
BF = jnp.bfloat16
F32 = jnp.float32
MESH = pl.DeviceIdType.MESH
X_ORDER = (0, 1, 3, 2)
FORWARD_PLUS = (0, 2, 5, 7)
FORWARD_MINUS = (1, 3, 4, 6)


def constants():
    perm = np.zeros((256, 256), np.float32)
    for z in range(8):
        for t in range(8):
            for r in range(4):
                perm[t * 32 + z * 4 + r, z * 32 + t * 4 + r] = 1
    col = np.arange(512)
    mask_in = np.zeros((128, 1024), np.float32)
    pick = np.zeros((1024, 128), np.float32)
    for k in range(2):
        mask_in[k * 8 + col // 64, k * 512 + col] = 1
        pick[k * 512 + col, (col % 2) * 64 + k * 32 + (col % 64) // 2] = 1
    gate = np.zeros((128, 128), np.float32)
    for k in range(2):
        for j in range(3):
            gate[16 + 3 * k + j, k * 32 : k * 32 + 32] = 1
    spread = np.zeros((2, 128, 512), np.float32)
    mask_out = np.zeros((128, 512), np.float32)
    unit = np.arange(256)
    for k in range(2):
        mask_out[k * 8 + unit // 32, k * 256 + unit] = 1
        for c in range(2):
            spread[c, c * 64 + k * 32 + unit % 32, k * 256 + unit] = 1
    repeat = np.zeros((128, 512), np.float32)
    repeat[((col // 32) % 8) * 16 + col % 16, col] = 1
    return [
        jnp.asarray(a, BF) for a in (perm, perm.T, mask_in, pick, gate, spread, mask_out, repeat)
    ]


def dot(a, b):
    return jnp.dot(a, b, preferred_element_type=F32)


def dot_nt(a, b):
    return lax.dot_general(a, b, (((1,), (1,)), ((), ())), preferred_element_type=F32)


def kernel(
    pieces, w_in, w_out, key_own, q_send,
    perm, perm_t, mask_in, pick, gate, spread, mask_out, repeat,
    out_rows, out_latent,
    got, rows, part, part_got, hid, share, share_sib, ring_out, ring_in, col_sum, col_got,
    back_out, back_got, keys, q_col, q_own, lat_own, lat_col, lat_got,
    s_piece, r_piece, s_ring, r_ring, s_x, r_x, s_fwd, r_fwd, s_sib, r_sib,
    s_part, r_part, s_hid, r_hid, s_ssib, r_ssib, s_red, r_red, s_col, r_col, s_back, r_back,
    s_key, r_key, s_ksib, r_ksib, s_qy, r_qy, s_qx, r_qx, s_ly, r_ly, s_lx, r_lx,
):
    z = lax.axis_index("dp")
    e = lax.axis_index("expert")
    c = lax.rem(e, 2)
    y = lax.rem(e // 2, NY)
    x = e // (2 * NY)
    sign = 1 - 2 * c

    def at_z(d):
        return lax.rem(z + d, NZ)

    def at_x(d):
        return lax.rem(x + d, NX)

    def at_y(d):
        return lax.rem(y + NY + d, NY)

    def on_z(d):
        return (at_z(d), e)

    def on_x(d):
        return (z, (at_x(d) * NY + y) * 2 + c)

    def on_y(d):
        return (z, (x * NY + at_y(d)) * 2 + c)

    sibling = (z, e + 1 - 2 * c)

    barrier = pltpu.get_barrier_semaphore()
    peers = [on_z(d) for d in range(1, NZ)] + [on_y(d) for d in range(1, NY)]
    peers += [on_x(d) for d in range(1, NX)] + [sibling]
    for peer in peers:
        pl.semaphore_signal(barrier, inc=1, device_id=peer, device_id_type=MESH)
    pl.semaphore_wait(barrier, len(peers))

    sent = []

    def send(src, dst, s_sem, r_sem, peer):
        copy = pltpu.make_async_remote_copy(
            src_ref=src, dst_ref=dst, send_sem=s_sem, recv_sem=r_sem,
            device_id=peer, device_id_type=MESH,
        )
        copy.start()
        sent.append(copy)
        return copy

    piece = [
        send(pieces.at[at_z(d)], got.at[z], s_piece.at[d - 1], r_piece.at[d - 1], on_z(d))
        for d in range(1, NZ)
    ]
    key_z = [
        send(key_own, keys.at[c, z], s_key.at[d - 1], r_key.at[d - 1], on_z(d))
        for d in range(1, NZ)
    ]
    q_y = [
        send(q_send.at[at_y(d)], q_col.at[y], s_qy.at[d - 1], r_qy.at[d - 1], on_y(d))
        for d in range(1, NY)
    ]
    got[z] = pieces[z]
    keys[c, z] = key_own[...]
    q_col[y] = q_send[y]

    for copy in piece:
        copy.wait_recv()
    turned = dot(perm[...], got[...].reshape(256, 128)).astype(BF)
    for t in range(8):
        rows[x, c, y, :, t * 128 : (t + 1) * 128] = turned[t * 32 : (t + 1) * 32]

    def block(xi, yi):
        return rows.at[xi, c, yi]

    origins, x_plus, x_minus = [], [], []

    def to_x(origin):
        k = len(origins)
        origins.append(origin)
        b = block(x, origin)
        x_plus.append(send(b, b, s_x.at[0, k], r_x.at[0, k], on_x(1)))
        x_minus.append(send(b, b, s_x.at[1, k], r_x.at[1, k], on_x(3)))

    def ring(origin, way, step):
        b = block(x, origin)
        peer = on_y(sign) if way == 0 else on_y(-sign)
        return send(b, b, s_ring.at[way, step], r_ring.at[way, step], peer)

    plus, minus = ring(y, 0, 0), ring(y, 1, 0)
    to_x(y)
    q_x = None
    for step in range(1, 5):
        plus.wait_recv()
        origin = at_y(-sign * step)
        if step < 4:
            plus = ring(origin, 0, step)
        to_x(origin)
        if step < 4:
            minus.wait_recv()
            origin = at_y(sign * step)
            if step < 3:
                minus = ring(origin, 1, step)
            to_x(origin)
        if step == 1:
            for copy in q_y:
                copy.wait_recv()
            q_x = [
                send(q_col.at[:, at_x(d)], q_own.at[x], s_qx.at[d - 1], r_qx.at[d - 1], on_x(d))
                for d in range(1, NX)
            ]
            q_own[x] = q_col[:, x]
        if step == 2:
            for copy in key_z:
                copy.wait_recv()
            key_sib = send(keys.at[c], keys.at[c], s_ksib.at[0], r_ksib.at[0], sibling)

    def to_sibling(j):
        b = rows.at[at_x(X_ORDER[j]), c]
        return send(b, b, s_sib.at[j], r_sib.at[j], sibling)

    def project(j):
        xi = at_x(X_ORDER[j])

        def body(ci, carry):
            routing = rows[xi, ci, :, :, 896:1024].reshape(256, 128)
            mask = dot(routing, mask_in[...])
            values = dot_nt(rows[xi, ci, :, :, 0:896].reshape(256, 896), w_in[...])
            first = (values * mask[:, :512]).astype(BF)
            second = (values * mask[:, 512:]).astype(BF)
            picked = dot(first, pick[0:512, :]) + dot(second, pick[512:1024, :])
            part[j, :, pl.ds(pl.multiple_of(ci * 32, 32), 32), :] = picked.astype(BF).reshape(
                8, 32, 128
            )
            return carry

        lax.fori_loop(0, 2, body, 0)
        return [
            send(
                part.at[j, at_z(d)], part_got.at[j, d - 1],
                s_part.at[j, d - 1], r_part.at[j, d - 1], on_z(d),
            )
            for d in range(1, NZ)
        ]

    def activate(j, arriving):
        xi = at_x(X_ORDER[j])
        for copy in arriving:
            copy.wait_recv()
        total = part[j, z].astype(F32)
        for d in range(7):
            total = total + part_got[j, d].astype(F32)
        up = pltpu.roll(total, 64, 1)
        routing = rows[xi, :, z, :, 896:1024].reshape(64, 128)
        value = total / (1.0 + jnp.exp(-total)) * up * dot(routing, gate[...])
        lane = lax.broadcasted_iota(jnp.int32, (32, 128), 1)
        packed = jnp.where(lane < 64, value[0:32], pltpu.roll(value[32:64], 64, 1))
        hid[j, z] = packed.astype(BF)
        return [
            send(
                hid.at[j, z], hid.at[j, z],
                s_hid.at[j, d - 1], r_hid.at[j, d - 1], on_z(d),
            )
            for d in range(1, NZ)
        ]

    def project_down(j, arriving):
        xi = at_x(X_ORDER[j])
        for copy in arriving:
            copy.wait_recv()

        def body(ci, carry):
            routing = rows[xi, ci, :, :, 896:1024].reshape(256, 128)
            wide = dot(hid[j].reshape(256, 128), spread[ci]) * dot(routing, mask_out[...])
            dense = (wide[:, :256] + wide[:, 256:]).astype(BF)
            share[j, ci] = dot(dense, w_out[...]).astype(BF).reshape(8, 32, 896)
            return carry

        lax.fori_loop(0, 2, body, 0)
        return send(
            share.at[j, 1 - c], share_sib.at[j], s_ssib.at[j], r_ssib.at[j], sibling
        )

    def own_share(j, target):
        return share[j, c, target].astype(F32) + share_sib[j, target].astype(F32)

    def reduce_step(j, step, state):
        new = [None, None]
        if step == 1:
            state.wait_recv()
        for way, hops in ((0, 4), (1, 3)):
            if step > hops:
                new[way] = state[way]
                continue
            target = at_y(sign * (hops + 1 - step) * (1 - 2 * way))
            value = own_share(j, target)
            if step > 1:
                state[way].wait_recv()
                value = value + ring_in[j, way, step - 2].astype(F32)
            ring_out[j, way, step - 1] = value.astype(BF)
            new[way] = send(
                ring_out.at[j, way, step - 1], ring_in.at[j, way, step - 1],
                s_red.at[j, way, step - 1], r_red.at[j, way, step - 1],
                on_y(sign * (1 - 2 * way)),
            )
        return new

    def reduce_end(j, state):
        state[0].wait_recv()
        state[1].wait_recv()
        value = own_share(j, y) + ring_in[j, 0, 3].astype(F32) + ring_in[j, 1, 2].astype(F32)
        col_sum[j] = value.astype(BF)
        if j == 0:
            return None
        return send(
            col_sum.at[j], col_got.at[j - 1], s_col.at[j - 1], r_col.at[j - 1], on_x(X_ORDER[j])
        )

    def absorb():
        for copy in q_x:
            copy.wait_recv()
        key_sib.wait_recv()
        wide = dot(q_own[...].reshape(512, 128), repeat[...])
        row = lax.broadcasted_iota(jnp.int32, (512, 512), 0)
        lane = lax.broadcasted_iota(jnp.int32, (512, 512), 1)
        head = (lane // 256) * 2 + (lane // 16) % 2
        wide = jnp.where(row % 4 == head, wide, 0.0).astype(BF)
        lat_own[...] = dot(wide, keys[...].reshape(512, 512)).astype(BF).reshape(4, 8, 16, 512)
        copies = [
            send(lat_own.at[:, at_y(d)], lat_col.at[y], s_ly.at[d - 1], r_ly.at[d - 1], on_y(d))
            for d in range(1, NY)
        ]
        lat_col[y] = lat_own[:, y]
        return copies

    def latent_x(arriving):
        for copy in arriving:
            copy.wait_recv()
        copies = [
            send(lat_col.at[:, at_x(d)], lat_got.at[x], s_lx.at[d - 1], r_lx.at[d - 1], on_x(d))
            for d in range(1, NX)
        ]
        lat_got[x] = lat_col[:, x]
        return copies

    sib = [to_sibling(0)]
    lat_y = absorb()
    sib[0].wait_recv()
    parts = [project(0)]
    far = []
    for k in range(8):
        x_minus[k].wait_recv()
        if k in FORWARD_MINUS:
            b = block(at_x(1), origins[k])
            far.append(send(b, b, s_fwd.at[k], r_fwd.at[k], on_x(3)))
        x_plus[k].wait_recv()
        if k in FORWARD_PLUS:
            b = block(at_x(3), origins[k])
            far.append(send(b, b, s_fwd.at[k], r_fwd.at[k], on_x(1)))
    sib.append(to_sibling(1))
    sib.append(to_sibling(2))
    hids = [activate(0, parts[0])]
    sib[1].wait_recv()
    parts.append(project(1))
    downs = [project_down(0, hids[0])]
    sib[2].wait_recv()
    parts.append(project(2))
    hids.append(activate(1, parts[1]))
    red = [reduce_step(0, 1, downs[0])]
    downs.append(project_down(1, hids[1]))
    hids.append(activate(2, parts[2]))
    red[0] = reduce_step(0, 2, red[0])
    red.append(reduce_step(1, 1, downs[1]))
    for copy in far:
        copy.wait_recv()
    sib.append(to_sibling(3))
    lat_x = latent_x(lat_y)
    downs.append(project_down(2, hids[2]))
    red[0] = reduce_step(0, 3, red[0])
    sib[3].wait_recv()
    parts.append(project(3))
    red[1] = reduce_step(1, 2, red[1])
    red.append(reduce_step(2, 1, downs[2]))
    red[0] = reduce_step(0, 4, red[0])
    hids.append(activate(3, parts[3]))
    red[1] = reduce_step(1, 3, red[1])
    red[2] = reduce_step(2, 2, red[2])
    downs.append(project_down(3, hids[3]))
    red.append(reduce_step(3, 1, downs[3]))
    red[1] = reduce_step(1, 4, red[1])
    red[2] = reduce_step(2, 3, red[2])
    red[3] = reduce_step(3, 2, red[3])
    reduce_end(0, red[0])
    cols = [reduce_end(1, red[1])]
    red[2] = reduce_step(2, 4, red[2])
    red[3] = reduce_step(3, 3, red[3])
    cols.append(reduce_end(2, red[2]))
    red[3] = reduce_step(3, 4, red[3])
    for copy in lat_x:
        copy.wait_recv()
    out_latent[...] = lat_got[...]
    cols.append(reduce_end(3, red[3]))

    total = col_sum[0].astype(F32)
    for j in range(3):
        cols[j].wait_recv()
        total = total + col_got[j].astype(F32)
    total = total.astype(BF)
    tiles = [total[:, t * 128 : (t + 1) * 128] for t in range(7)] + [jnp.zeros((32, 128), BF)]
    tiles = jnp.concatenate(tiles, axis=0)
    back_out[...] = dot(perm_t[...], tiles).astype(BF).reshape(8, 32, 128)
    back = [
        send(back_out.at[at_z(d)], back_got.at[z], s_back.at[d - 1], r_back.at[d - 1], on_z(d))
        for d in range(1, NZ)
    ]
    back_got[z] = back_out[z]
    for copy in back:
        copy.wait_recv()
    out_rows[...] = back_got[...]
    for copy in sent:
        copy.wait_send()


def exchange(pieces, w_in, w_out, key_own, q_send):
    dma = pltpu.SemaphoreType.DMA
    sems = [
        (7,), (2, 4), (2, 8), (8,), (4,),
        (4, 7), (4, 7), (4,), (4, 2, 4), (3,), (7,),
        (7,), (1,), (7,), (3,), (7,), (3,),
    ]
    vmem = pl.BlockSpec(memory_space=pltpu.VMEM)
    consts = constants()
    return pl.pallas_call(
        kernel,
        out_shape=(
            jax.ShapeDtypeStruct((8, 32, 128), BF),
            jax.ShapeDtypeStruct((4, 8, 16, 512), BF),
        ),
        in_specs=[vmem] * (5 + len(consts)),
        out_specs=(vmem, vmem),
        scratch_shapes=[
            pltpu.VMEM((8, 32, 128), BF),
            pltpu.VMEM((4, 2, 8, 32, 1024), BF),
            pltpu.VMEM((4, 8, 64, 128), BF),
            pltpu.VMEM((4, 7, 64, 128), BF),
            pltpu.VMEM((4, 8, 32, 128), BF),
            pltpu.VMEM((4, 2, 8, 32, 896), BF),
            pltpu.VMEM((4, 8, 32, 896), BF),
            pltpu.VMEM((4, 2, 4, 32, 896), BF),
            pltpu.VMEM((4, 2, 4, 32, 896), BF),
            pltpu.VMEM((4, 32, 896), BF),
            pltpu.VMEM((3, 32, 896), BF),
            pltpu.VMEM((8, 32, 128), BF),
            pltpu.VMEM((8, 32, 128), BF),
            pltpu.VMEM((2, 8, 32, 512), BF),
            pltpu.VMEM((8, 4, 16, 128), BF),
            pltpu.VMEM((4, 8, 16, 128), BF),
            pltpu.VMEM((4, 8, 16, 512), BF),
            pltpu.VMEM((8, 4, 16, 512), BF),
            pltpu.VMEM((4, 8, 16, 512), BF),
        ]
        + [dma(shape) for shape in sems for _ in range(2)],
        compiler_params=pltpu.CompilerParams(
            collective_id=0, has_side_effects=True, vmem_limit_bytes=48 * 1024 * 1024
        ),
        cost_estimate=pl.CostEstimate(
            flops=6_000_000_000, bytes_accessed=8_000_000, transcendentals=500_000
        ),
    )(pieces, w_in, w_out, key_own, q_send, *consts)


def on_device(
    query_nope,
    query_rope,
    latent_cache,
    key_rope,
    lengths,
    key_weight,
    expert_input,
    route_slots,
    route_gates,
    trainer_gate_up,
    trainer_down,
    trainer_order,
    rollout_order,
):
    named = route_slots[:, :, None] == jnp.arange(8, dtype=jnp.int32)[None, None, :]
    expert = jnp.sum(jnp.where(named, rollout_order[None, None, :], 0), axis=2)
    one_hot = (expert[:, :, None] == trainer_order[None, None, :]).astype(F32)
    high = lax.reduce_precision(route_gates, 8, 7)
    middle = lax.reduce_precision(route_gates - high, 8, 7)
    low = lax.reduce_precision(route_gates - high - middle, 8, 7)
    gates = jnp.stack([high, middle, low], axis=2).reshape(4, 6)
    routing = jnp.concatenate(
        [one_hot.reshape(4, 16), gates, jnp.zeros((4, 106), F32)], axis=1
    ).astype(BF)
    pieces = expert_input.reshape(4, 8, 7, 128).transpose(1, 2, 0, 3)
    routing = jnp.broadcast_to(routing[None, None], (8, 1, 4, 128))
    pieces = jnp.concatenate([pieces, routing], axis=1).reshape(8, 32, 128)
    q_send = query_nope.reshape(4, NX, NY, 4, NOPE).transpose(2, 1, 0, 3, 4).reshape(8, 4, 16, 128)
    out_rows, latent = exchange(
        pieces,
        trainer_gate_up.reshape(512, 896),
        trainer_down.reshape(256, 896),
        key_weight.reshape(32, 512),
        q_send,
    )
    expert_output = (
        out_rows.reshape(8, 8, 4, 128)[:, :7].transpose(2, 0, 1, 3).reshape(4, 7168)
    )
    query_latent = latent.reshape(32, 4, 4, 512).transpose(1, 0, 2, 3).reshape(4, 128, 512)

    score_scale = 1.0 / math.sqrt(NOPE + ROPE)
    scores = jnp.einsum("rhk,rlk->rhl", query_latent, latent_cache, preferred_element_type=F32)
    scores = scores + jnp.einsum(
        "rhp,rlp->rhl", query_rope, key_rope, preferred_element_type=F32
    )
    scores = scores * score_scale
    visible = (
        jnp.arange(latent_cache.shape[1], dtype=jnp.int32)[None, None, :] < lengths[:, None, None]
    )
    scores = jnp.where(visible, scores, -jnp.inf)
    highest = jnp.max(scores, axis=2, keepdims=True)
    raised = jnp.exp(scores - highest)
    attention = (raised / jnp.sum(raised, axis=2, keepdims=True)).astype(BF)
    latent_output = jnp.einsum(
        "rhl,rlk->rhk", attention, latent_cache, preferred_element_type=F32
    ).astype(BF)
    return (latent_output, expert_output)


def solution(mesh):
    in_specs = (
        P(("dp", "expert"), None, None),
        P(("dp", "expert"), None, None),
        P(("dp", "expert"), None, None),
        P(("dp", "expert"), None, None),
        P(("dp", "expert")),
        P("expert", "dp", None),
        P(("dp", "expert"), None),
        P(("dp", "expert"), None),
        P(("dp", "expert"), None),
        P(None, "expert", None, "dp"),
        P(None, "expert", "dp"),
        P(),
        P(),
    )
    out_specs = (P(("dp", "expert"), None, None), P(("dp", "expert"), None))
    return jax.shard_map(
        on_device, mesh=mesh, in_specs=in_specs, out_specs=out_specs, check_vma=False
    )
```

time: 482 us -> 129 us (0.27); the launches traced: 474 us -> 127 us
  waiting for transfers between devices: 285 us -> 0 us
  Pallas kernels: 0 us -> 105 us
  local copies, waits for them, and re-layouts: 71.6 us -> 16.1 us
  starting transfers between devices: 53.5 us -> 0 us
  blocking collectives: 24.9 us -> 0 us
  matrix products: 19.7 us -> 2.99 us
  between operations: 14.5 us -> 0.83 us
    all_to_all x6 -> x0, waiting for transfers between devices: 176 us -> none  [the longest x1 123 us: on_device(): lax.all_to_all(placed_gates, 'expert', split_axis=0, concat_axis=0, tiled...]
    all_gather x2 -> x0, waiting for transfers between devices: 108 us -> none  [the longest x1 79.9 us: on_device(): lax.all_gather(trainer_gate_up, 'dp', axis=3, tiled=True)]
    pallas_call x0 -> x1, Pallas kernels: none -> 105 us  [exchange(): pl.pallas_call(kernel, out_shape=(jax.ShapeDtypeStruct((8, 32, 128), BF),...]
    all_to_all x6 -> x0, starting transfers between devices: 53.5 us -> none  [the longest x1 10.8 us: on_device(): lax.all_to_all(query_send, 'expert', split_axis=1, concat_axis=0, tiled=T...]
    reshape x7 -> x6, local copies, waits for them, and re-layouts: 44.8 us -> 4.3 us  [the longest x1 2.45 us: on_device(): trainer_gate_up.reshape(512, 896)]
    all_gather x1 -> x0, blocking collectives: 24.9 us -> none  [on_device(): lax.all_gather(key_weight, 'dp', axis=1, tiled=True)]
    dot_general x8 -> x1, matrix products: 17 us -> 0.34 us  [on_device(): jnp.einsum('rhp,rlp->rhl', query_rope, key_rope, preferred_element_type=F32)]
    all_gather x2 -> x0, local copies, waits for them, and re-layouts: 13.2 us -> none  [the longest x1 9.12 us: on_device(): lax.all_gather(trainer_gate_up, 'dp', axis=3, tiled=True)]
  transfers between devices with their start and end apart: 8 -> 0, of which waited for: 7 -> 0; matrix products, arithmetic and copies ran while one was open for 19% -> 0% of each run, Pallas kernels for 0% -> 0%
where the time goes in v1:
time: 129 us; the launch traced here: 127 us
  Pallas kernels  105 us (81%)
  local copies, waits for them, and re-layouts  16.1 us (12%)
  matrix products  2.99 us (2%)
  other arithmetic  2.27 us (2%)
    pallas_call x1, Pallas kernels, exchange(): pl.pallas_call(kernel, out_shape=(jax.ShapeDtypeStruct((8, 32, 128), BF),...  105 us
    unnamed x35, local copies, waits for them, and re-layouts  9.62 us

profile of v1, /device:TPU:6, one launch (start us, length us, event | category | flops | bytes accessed | tf_op | source)
XLA Modules:
  0.0 127.3 jit_solution(122579506917653959)
XLA Ops:
  0.7 0.9 fusion.8
  1.5 0.1 copy.36
  1.6 0.1 concatenate.13
  1.7 0.9 select_reduce_fusion
  2.6 0.1 copy.35
  2.8 0.1 eq.39
  2.9 0.7 eq.40
  3.5 0.1 eq.41
  3.7 0.1 maximum_maximum_fusion
  3.8 0.9 reshape.102
  4.8 0.7 copy.37
  5.4 2.5 %reshape.104.w_in = bf16[512,896]{1,0:T(8,128)(2,1)S(1)} reshape(bf16[8,32,2,896]{3,2,1,0:T(2,128)(2,1)} %param.30) | data formatting | bytes 1835008 | tf_op jit(solution)/shard_map/reshape | solution.py:467
  8.0 0.8 copy-done.1
  8.8 1.0 copy-done.4
  9.8 0.8 copy-done.5
  10.6 0.9 copy-done.6
  11.5 0.9 copy-done.7
  12.5 0.9 copy-done.8
  13.4 0.9 copy-done.9
  14.4 0.9 copy-done.10
  15.3 0.9 copy-done.11
  16.2 0.8 copy-done.12
  16.9 105.1 %shard_map.212 = (bf16[8,32,128]{2,1,0:T(8,128)(2,1)S(1)}, bf16[4,8,16,512]{3,2,1,0:T(8,128)(2,1)S(1)}) custom-call(bf16[8,32,128]{2,1,0:T(8,128)(2,1)S(1)} %bitcast.29, bf16[512,896]{1,0:T(8,128)(2,1)S(1)} %reshape.104.w_in, bf16[256,896]{1,0:T(8,128)(2,1)S(1)} %bitcast.31, bf16[32,512]{1,0:T(8,128)(2,1)S(1)} %bitcast.32, ...), custom_call_target="tpu_custom_call" | custom-call | flops 6000000000 | bytes 8000000 | tf_op jit(solution)/shard_map/pallas_call | solution.py:397
  122.0 0.6 copy-done.2
  122.6 0.1 reshape.109
  122.8 0.2 copy.39
  123.0 0.1 reshape.110
  123.1 0.8 fusion.13
  124.1 0.3 fusion.4
  124.4 0.3 fusion.12
  124.7 1.8 %convolution_convert_fusion = bf16[4,128,512]{2,1,0:T(8,128)(2,1)} fusion(bf16[4,512,512]{2,1,0:T(8,128)(2,1)S(1)} %copy-done, f32[4,128]{1,0:T(4,128)S(1)} %fusion.12, f32[4,128,512]{2,1,0:T(8,128)S(1)} %fusion.4), kind=kOutput, calls=%fused_computation.6 | convolution fusion | flops 269485056 | bytes 3672064 | tf_op jit(solution)/shard_map/rhl,rlk->rhk/dot_general | solution.py:490
  126.6 0.7 reshape.112
  (34 shorter events, 0.5 us)
Async XLA Ops:
  0.6 122.5 %copy-start = (bf16[4,512,512]{2,1,0:T(8,128)(2,1)S(1)}, bf16[4,512,512]{2,1,0:T(8,128)(2,1)}, u32[]{:S(2)}) copy-start(bf16[4,512,512]{2,1,0:T(8,128)(2,1)} %param.23) | copy-start | bytes 6291460
  0.6 7.3 %copy-start.14 = (bf16[4,128,128]{2,1,0:T(8,128)(2,1)S(1)}, bf16[4,128,128]{2,1,0:T(8,128)(2,1)}, u32[]{:S(2)}) copy-start(bf16[4,128,128]{2,1,0:T(8,128)(2,1)} %param.21) | copy-start | bytes 393220
  8.0 0.8 copy-start.1
  8.8 1.0 copy-start.4
  9.8 0.8 copy-start.5
  10.6 0.9 copy-start.6
  11.5 0.9 copy-start.7
  12.5 0.9 copy-start.8
  13.4 0.9 copy-start.9
  14.4 0.9 copy-start.10
  15.3 0.9 copy-start.11
  16.2 0.8 copy-start.12
  122.0 0.6 copy-start.2
  123.0 1.0 copy-start.16
  123.1 1.0 copy-start.13
  123.1 0.9 copy-start.15
  124.7 1.9 %copy-start.3 = (bf16[8,32,128]{2,1,0:T(8,128)(2,1)S(1)}, bf16[8,32,128]{2,1,0:T(8,128)(2,1)}, u32[]{:S(2)}) copy-start(bf16[8,32,128]{2,1,0:T(8,128)(2,1)} %copy-done.2) | copy-start | bytes 196612

commit v2 on v1

v2 whole, which is shorter than its diff:
```python
import math

import jax
import jax.numpy as jnp
import numpy as np
from jax import lax
from jax.experimental import pallas as pl
from jax.experimental.pallas import tpu as pltpu
from jax.sharding import PartitionSpec as P

NOPE = 128
ROPE = 64
NX, NY, NZ = 4, 8, 8
BF = jnp.bfloat16
F32 = jnp.float32
MESH = pl.DeviceIdType.MESH
SCORE_SCALE = 1.0 / math.sqrt(NOPE + ROPE)
X_ORDER = (0, 1, 3, 2)
FORWARD_PLUS = (0, 2, 5, 7)
FORWARD_MINUS = (1, 3, 4, 6)


def constants():
    perm = np.zeros((256, 256), np.float32)
    for z in range(8):
        for t in range(8):
            for r in range(4):
                perm[t * 32 + z * 4 + r, z * 32 + t * 4 + r] = 1
    col = np.arange(512)
    mask_in = np.zeros((128, 1024), np.float32)
    pick = np.zeros((1024, 128), np.float32)
    for k in range(2):
        mask_in[k * 8 + col // 64, k * 512 + col] = 1
        pick[k * 512 + col, (col % 2) * 64 + k * 32 + (col % 64) // 2] = 1
    gate = np.zeros((128, 128), np.float32)
    for k in range(2):
        for j in range(3):
            gate[16 + 3 * k + j, k * 32 : k * 32 + 32] = 1
    spread = np.zeros((2, 128, 512), np.float32)
    mask_out = np.zeros((128, 512), np.float32)
    unit = np.arange(256)
    for k in range(2):
        mask_out[k * 8 + unit // 32, k * 256 + unit] = 1
        for c in range(2):
            spread[c, c * 64 + k * 32 + unit % 32, k * 256 + unit] = 1
    repeat = np.zeros((128, 512), np.float32)
    repeat[((col // 32) % 8) * 16 + col % 16, col] = 1
    by_row = np.zeros((512, 512), np.float32)
    by_row[((col // 4) % 4) * 128 + (col // 16) * 4 + col % 4, col] = 1
    return [
        jnp.asarray(a, BF)
        for a in (perm, perm.T, mask_in, pick, gate, spread, mask_out, repeat, by_row)
    ]


def dot(a, b):
    return jnp.dot(a, b, preferred_element_type=F32)


def dot_nt(a, b):
    return lax.dot_general(a, b, (((1,), (1,)), ((), ())), preferred_element_type=F32)


def kernel(
    x_hbm, slots_hbm, gates_hbm, trainer_hbm, rollout_hbm, w_raw_hbm, w_out_hbm, key_hbm, q_hbm,
    cache_hbm, q_rope_hbm, k_rope_hbm, lengths_hbm,
    perm_hbm, perm_t_hbm, mask_in_hbm, pick_hbm, gate_hbm, spread_hbm, mask_out_hbm, repeat_hbm,
    by_row_hbm,
    out_rows, out_latent,
    x_in, slots, gates, trainer, rollout, w_raw, w_out, key_own, q_send,
    cache, q_rope, k_rope, lengths,
    perm, perm_t, mask_in, pick, gate, spread, mask_out, repeat, by_row,
    pieces, w_in, lat_rows, s_load,
    got, rows, part, part_got, hid, share, share_sib, ring_out, ring_in, col_sum, col_got,
    back_out, back_got, keys, q_col, q_own, lat_own, lat_col, lat_got,
    s_piece, r_piece, s_ring, r_ring, s_x, r_x, s_fwd, r_fwd, s_sib, r_sib,
    s_part, r_part, s_hid, r_hid, s_ssib, r_ssib, s_red, r_red, s_col, r_col, s_back, r_back,
    s_key, r_key, s_ksib, r_ksib, s_qy, r_qy, s_qx, r_qx, s_ly, r_ly, s_lx, r_lx,
):
    z = lax.axis_index("dp")
    e = lax.axis_index("expert")
    c = lax.rem(e, 2)
    y = lax.rem(e // 2, NY)
    x = e // (2 * NY)
    sign = 1 - 2 * c

    def at_z(d):
        return lax.rem(z + d, NZ)

    def at_x(d):
        return lax.rem(x + d, NX)

    def at_y(d):
        return lax.rem(y + NY + d, NY)

    def on_z(d):
        return (at_z(d), e)

    def on_x(d):
        return (z, (at_x(d) * NY + y) * 2 + c)

    def on_y(d):
        return (z, (x * NY + at_y(d)) * 2 + c)

    sibling = (z, e + 1 - 2 * c)

    loads = [
        pltpu.make_async_copy(src, dst, s_load.at[i])
        for i, (src, dst) in enumerate(
            (
                (x_hbm, x_in), (slots_hbm, slots), (gates_hbm, gates),
                (trainer_hbm, trainer), (rollout_hbm, rollout),
                (key_hbm, key_own), (q_hbm, q_send), (perm_hbm, perm),
                (w_raw_hbm, w_raw), (repeat_hbm, repeat),
                (mask_in_hbm, mask_in), (pick_hbm, pick), (gate_hbm, gate),
                (spread_hbm, spread), (mask_out_hbm, mask_out), (w_out_hbm, w_out),
                (perm_t_hbm, perm_t),
                (by_row_hbm, by_row), (lengths_hbm, lengths), (cache_hbm, cache),
                (q_rope_hbm, q_rope), (k_rope_hbm, k_rope),
            )
        )
    ]
    for load in loads:
        load.start()

    barrier = pltpu.get_barrier_semaphore()
    peers = [on_z(d) for d in range(1, NZ)] + [on_y(d) for d in range(1, NY)]
    peers += [on_x(d) for d in range(1, NX)] + [sibling]
    for peer in peers:
        pl.semaphore_signal(barrier, inc=1, device_id=peer, device_id_type=MESH)

    for load in loads[:5]:
        load.wait()
    lane = lax.broadcasted_iota(jnp.int32, (8, 128), 1)
    row = lax.broadcasted_iota(jnp.int32, (8, 128), 0)
    trainer_lane = jnp.zeros((8, 128), jnp.int32)
    for i in range(8):
        trainer_lane = jnp.where(lane % 8 == i, trainer[i], trainer_lane)
    expert = jnp.full((8, 128), -1, jnp.int32)
    gate_lane = jnp.zeros((8, 128), F32)
    for r in range(4):
        for k in range(2):
            expert = jnp.where((row == r) & (lane // 8 == k), rollout[slots[k, r]], expert)
            term = (lane >= 16 + 3 * k) & (lane < 19 + 3 * k)
            gate_lane = jnp.where((row == r) & term, gates[k, r], gate_lane)
    high = gate_lane.astype(BF).astype(F32)
    middle = (gate_lane - high).astype(BF).astype(F32)
    low = gate_lane - high - middle
    term = (lane + 2) % 3
    routing = jnp.where(expert == trainer_lane, 1.0, 0.0)
    routing = routing + jnp.where(term == 0, high, jnp.where(term == 1, middle, low))
    own_rows = x_in[...].astype(F32)
    for d in range(NZ):
        tiles = [own_rows[d * 28 : (d + 1) * 28], routing[0:4]]
        pieces[d] = jnp.concatenate(tiles, axis=0).astype(BF)
    pl.semaphore_wait(barrier, len(peers))

    sent = []

    def send(src, dst, s_sem, r_sem, peer):
        copy = pltpu.make_async_remote_copy(
            src_ref=src, dst_ref=dst, send_sem=s_sem, recv_sem=r_sem,
            device_id=peer, device_id_type=MESH,
        )
        copy.start()
        sent.append(copy)
        return copy

    piece = [
        send(pieces.at[at_z(d)], got.at[z], s_piece.at[d - 1], r_piece.at[d - 1], on_z(d))
        for d in range(1, NZ)
    ]
    loads[6].wait()
    q_y = [
        send(q_send.at[at_y(d)], q_col.at[y], s_qy.at[d - 1], r_qy.at[d - 1], on_y(d))
        for d in range(1, NY)
    ]
    got[z] = pieces[z]
    q_col[y] = q_send[y]
    loads[5].wait()
    keys[c, z] = key_own[...]

    loads[7].wait()
    for copy in piece:
        copy.wait_recv()
    turned = dot(perm[...], got[...].reshape(256, 128)).astype(BF)
    for t in range(8):
        rows[x, c, y, :, t * 128 : (t + 1) * 128] = turned[t * 32 : (t + 1) * 32]

    def block(xi, yi):
        return rows.at[xi, c, yi]

    origins, x_plus, x_minus, far = [], [], [], []

    def to_x(origin):
        k = len(origins)
        origins.append(origin)
        b = block(x, origin)
        x_plus.append(send(b, b, s_x.at[0, k], r_x.at[0, k], on_x(1)))
        x_minus.append(send(b, b, s_x.at[1, k], r_x.at[1, k], on_x(3)))

    def pass_on(k):
        x_minus[k].wait_recv()
        if k in FORWARD_MINUS:
            b = block(at_x(1), origins[k])
            far.append(send(b, b, s_fwd.at[k], r_fwd.at[k], on_x(3)))
        x_plus[k].wait_recv()
        if k in FORWARD_PLUS:
            b = block(at_x(3), origins[k])
            far.append(send(b, b, s_fwd.at[k], r_fwd.at[k], on_x(1)))

    def ring(origin, way, step):
        b = block(x, origin)
        peer = on_y(sign) if way == 0 else on_y(-sign)
        return send(b, b, s_ring.at[way, step], r_ring.at[way, step], peer)

    plus, minus = ring(y, 0, 0), ring(y, 1, 0)
    to_x(y)
    key_z = [
        send(key_own, keys.at[c, z], s_key.at[d - 1], r_key.at[d - 1], on_z(d))
        for d in range(1, NZ)
    ]
    for copy in q_y:
        copy.wait_recv()
    q_x = [
        send(q_col.at[:, at_x(d)], q_own.at[x], s_qx.at[d - 1], r_qx.at[d - 1], on_x(d))
        for d in range(1, NX)
    ]
    q_own[x] = q_col[:, x]
    for step in range(1, 5):
        plus.wait_recv()
        origin = at_y(-sign * step)
        if step < 4:
            plus = ring(origin, 0, step)
        to_x(origin)
        if step < 4:
            minus.wait_recv()
            origin = at_y(sign * step)
            if step < 3:
                minus = ring(origin, 1, step)
            to_x(origin)
        if step == 1:
            loads[8].wait()

            def line_up(i, carry):
                start = pl.multiple_of(i * 64, 64)
                w_in[pl.ds(start, 64), :] = w_raw[i].reshape(64, 896)
                return carry

            lax.fori_loop(0, 8, line_up, 0)
        if step == 2:
            for load in loads[9:]:
                load.wait()
            pass_on(0)
        if step == 3:
            pass_on(1)
            pass_on(2)
            for copy in key_z:
                copy.wait_recv()
            key_sib = send(keys.at[c], keys.at[c], s_ksib.at[0], r_ksib.at[0], sibling)

    def to_sibling(j):
        b = rows.at[at_x(X_ORDER[j]), c]
        return send(b, b, s_sib.at[j], r_sib.at[j], sibling)

    def project(group):
        for j in group:
            xi = at_x(X_ORDER[j])

            def body(ci, carry):
                routing = rows[xi, ci, :, :, 896:1024].reshape(256, 128)
                mask = dot(routing, mask_in[...])
                values = dot_nt(rows[xi, ci, :, :, 0:896].reshape(256, 896), w_in[...])
                first = (values * mask[:, :512]).astype(BF)
                second = (values * mask[:, 512:]).astype(BF)
                picked = dot(first, pick[0:512, :]) + dot(second, pick[512:1024, :])
                picked = picked.astype(BF).reshape(8, 32, 128)
                part[:, j, pl.ds(pl.multiple_of(ci * 32, 32), 32), :] = picked
                return carry

            lax.fori_loop(0, 2, body, 0)
        js = pl.ds(group[0], len(group))
        return [
            send(
                part.at[at_z(d), js], part_got.at[d - 1, js],
                s_part.at[group[0], d - 1], r_part.at[group[0], d - 1], on_z(d),
            )
            for d in range(1, NZ)
        ]

    def activate(group, arriving):
        for copy in arriving:
            copy.wait_recv()
        for j in group:
            xi = at_x(X_ORDER[j])
            total = part[z, j].astype(F32)
            for d in range(7):
                total = total + part_got[d, j].astype(F32)
            up = pltpu.roll(total, 64, 1)
            routing = rows[xi, :, z, :, 896:1024].reshape(64, 128)
            value = total / (1.0 + jnp.exp(-total)) * up * dot(routing, gate[...])
            lane = lax.broadcasted_iota(jnp.int32, (32, 128), 1)
            packed = jnp.where(lane < 64, value[0:32], pltpu.roll(value[32:64], 64, 1))
            hid[z, j] = packed.astype(BF)
        js = pl.ds(group[0], len(group))
        return [
            send(
                hid.at[z, js], hid.at[z, js],
                s_hid.at[group[0], d - 1], r_hid.at[group[0], d - 1], on_z(d),
            )
            for d in range(1, NZ)
        ]

    def project_down(group, arriving):
        for copy in arriving:
            copy.wait_recv()
        copies = []
        for j in group:
            xi = at_x(X_ORDER[j])

            def body(i, carry):
                ci = lax.rem(1 - c + i, 2)
                routing = rows[xi, ci, :, :, 896:1024].reshape(256, 128)
                wide = dot(hid[:, j].reshape(256, 128), spread[ci]) * dot(routing, mask_out[...])
                dense = (wide[:, :256] + wide[:, 256:]).astype(BF)
                share[j, ci] = dot(dense, w_out[...]).astype(BF).reshape(8, 32, 896)
                return carry

            lax.fori_loop(0, 2, body, 0)
            copies.append(
                send(share.at[j, 1 - c], share_sib.at[j], s_ssib.at[j], r_ssib.at[j], sibling)
            )
        return copies

    def own_share(j, target):
        return share[j, c, target].astype(F32) + share_sib[j, target].astype(F32)

    def reduce_step(group, step, state):
        new = [None, None]
        if step == 1:
            for copy in state:
                copy.wait_recv()
        js = pl.ds(group[0], len(group))
        for way, hops in ((0, 4), (1, 3)):
            if step > hops:
                new[way] = state[way]
                continue
            target = at_y(sign * (hops + 1 - step) * (1 - 2 * way))
            if step > 1:
                state[way].wait_recv()
            for j in group:
                value = own_share(j, target)
                if step > 1:
                    value = value + ring_in[way, step - 2, j].astype(F32)
                ring_out[way, step - 1, j] = value.astype(BF)
            new[way] = send(
                ring_out.at[way, step - 1, js], ring_in.at[way, step - 1, js],
                s_red.at[group[0], way, step - 1], r_red.at[group[0], way, step - 1],
                on_y(sign * (1 - 2 * way)),
            )
        return new

    def reduce_end(group, state):
        state[0].wait_recv()
        state[1].wait_recv()
        copies = []
        for j in group:
            value = own_share(j, y) + ring_in[0, 3, j].astype(F32) + ring_in[1, 2, j].astype(F32)
            col_sum[j] = value.astype(BF)
            if j > 0:
                copies.append(
                    send(
                        col_sum.at[j], col_got.at[j - 1],
                        s_col.at[j - 1], r_col.at[j - 1], on_x(X_ORDER[j]),
                    )
                )
        return copies

    def absorb():
        for copy in q_x:
            copy.wait_recv()
        key_sib.wait_recv()
        wide = dot(q_own[...].reshape(512, 128), repeat[...])
        row = lax.broadcasted_iota(jnp.int32, (512, 512), 0)
        lane = lax.broadcasted_iota(jnp.int32, (512, 512), 1)
        head = (lane // 256) * 2 + (lane // 16) % 2
        wide = jnp.where(row % 4 == head, wide, 0.0).astype(BF)
        lat_own[...] = dot(wide, keys[...].reshape(512, 512)).astype(BF).reshape(4, 8, 16, 512)
        copies = [
            send(lat_own.at[:, at_y(d)], lat_col.at[y], s_ly.at[d - 1], r_ly.at[d - 1], on_y(d))
            for d in range(1, NY)
        ]
        lat_col[y] = lat_own[:, y]
        return copies

    def latent_x(arriving):
        for copy in arriving:
            copy.wait_recv()
        copies = [
            send(lat_col.at[:, at_x(d)], lat_got.at[x], s_lx.at[d - 1], r_lx.at[d - 1], on_x(d))
            for d in range(1, NX)
        ]
        lat_got[x] = lat_col[:, x]
        return copies

    def latent_end(arriving):
        for copy in arriving:
            copy.wait_recv()
        turned = dot(by_row[...], lat_got[...].reshape(512, 512)).astype(BF)
        lat_rows[...] = turned.reshape(4, 128, 512)

    def attend(r):
        scores = dot_nt(lat_rows[r], cache[r])
        scores = scores + lax.dot_general(
            q_rope[r], k_rope[r], (((0,), (0,)), ((), ())), preferred_element_type=F32
        )
        scores = scores * SCORE_SCALE
        place = lax.broadcasted_iota(jnp.int32, (128, 512), 1)
        scores = jnp.where(place < lengths[r], scores, -jnp.inf)
        raised = jnp.exp(scores - jnp.max(scores, axis=1, keepdims=True))
        attention = (raised / jnp.sum(raised, axis=1, keepdims=True)).astype(BF)
        out_latent[r] = dot(attention, cache[r]).astype(BF)

    one, two, three = (0,), (1, 2), (3,)
    sib = [to_sibling(0)]
    lat_y = absorb()
    sib[0].wait_recv()
    part_1 = project(one)
    for k in range(3, 8):
        pass_on(k)
    sib.append(to_sibling(1))
    sib.append(to_sibling(2))
    sib[1].wait_recv()
    sib[2].wait_recv()
    part_2 = project(two)
    hid_1 = activate(one, part_1)
    for copy in far:
        copy.wait_recv()
    sib.append(to_sibling(3))
    sib[3].wait_recv()
    part_3 = project(three)
    down_1 = project_down(one, hid_1)
    hid_2 = activate(two, part_2)
    lat_x = latent_x(lat_y)
    red_1 = reduce_step(one, 1, down_1)
    hid_3 = activate(three, part_3)
    down_2 = project_down(two, hid_2)
    red_1 = reduce_step(one, 2, red_1)
    down_3 = project_down(three, hid_3)
    red_2 = reduce_step(two, 1, down_2)
    red_1 = reduce_step(one, 3, red_1)
    red_3 = reduce_step(three, 1, down_3)
    red_1 = reduce_step(one, 4, red_1)
    latent_end(lat_x)
    red_2 = reduce_step(two, 2, red_2)
    red_3 = reduce_step(three, 2, red_3)
    attend(0)
    red_2 = reduce_step(two, 3, red_2)
    red_3 = reduce_step(three, 3, red_3)
    reduce_end(one, red_1)
    attend(1)
    red_2 = reduce_step(two, 4, red_2)
    red_3 = reduce_step(three, 4, red_3)
    attend(2)
    cols = reduce_end(two, red_2)
    cols += reduce_end(three, red_3)
    attend(3)

    total = col_sum[0].astype(F32)
    for j in range(3):
        cols[j].wait_recv()
        total = total + col_got[j].astype(F32)
    total = total.astype(BF)
    tiles = [total[:, t * 128 : (t + 1) * 128] for t in range(7)] + [jnp.zeros((32, 128), BF)]
    tiles = jnp.concatenate(tiles, axis=0)
    back_out[...] = dot(perm_t[...], tiles).astype(BF).reshape(8, 32, 128)
    back = [
        send(back_out.at[at_z(d)], back_got.at[z], s_back.at[d - 1], r_back.at[d - 1], on_z(d))
        for d in range(1, NZ)
    ]
    back_got[z] = back_out[z]
    for copy in back:
        copy.wait_recv()
    for d in range(NZ):
        part_rows = back_got[d].astype(F32)
        for t in range(7):
            first = (d * 7 + t) * 128
            out_rows[:, first : first + 128] = part_rows[t * 4 : t * 4 + 4].astype(BF)
    for copy in sent:
        copy.wait_send()


def exchange(*operands):
    dma = pltpu.SemaphoreType.DMA
    sems = [
        (7,), (2, 4), (2, 8), (8,), (4,),
        (4, 7), (4, 7), (4,), (4, 2, 4), (3,), (7,),
        (7,), (1,), (7,), (3,), (7,), (3,),
    ]
    vmem = pl.BlockSpec(memory_space=pltpu.VMEM)
    operands = list(operands) + constants()
    smem = (1, 2, 3, 4, 12)
    landing = [
        (pltpu.SMEM if i in smem else pltpu.VMEM)(a.shape, a.dtype) for i, a in enumerate(operands)
    ]
    return pl.pallas_call(
        kernel,
        out_shape=(
            jax.ShapeDtypeStruct((4, 7168), BF),
            jax.ShapeDtypeStruct((4, 128, 512), BF),
        ),
        in_specs=[pl.BlockSpec(memory_space=pltpu.HBM)] * len(operands),
        out_specs=(vmem, vmem),
        scratch_shapes=landing
        + [
            pltpu.VMEM((8, 32, 128), BF),
            pltpu.VMEM((512, 896), BF),
            pltpu.VMEM((4, 128, 512), BF),
            dma((len(operands),)),
            pltpu.VMEM((8, 32, 128), BF),
            pltpu.VMEM((4, 2, 8, 32, 1024), BF),
            pltpu.VMEM((8, 4, 64, 128), BF),
            pltpu.VMEM((7, 4, 64, 128), BF),
            pltpu.VMEM((8, 4, 32, 128), BF),
            pltpu.VMEM((4, 2, 8, 32, 896), BF),
            pltpu.VMEM((4, 8, 32, 896), BF),
            pltpu.VMEM((2, 4, 4, 32, 896), BF),
            pltpu.VMEM((2, 4, 4, 32, 896), BF),
            pltpu.VMEM((4, 32, 896), BF),
            pltpu.VMEM((3, 32, 896), BF),
            pltpu.VMEM((8, 32, 128), BF),
            pltpu.VMEM((8, 32, 128), BF),
            pltpu.VMEM((2, 8, 32, 512), BF),
            pltpu.VMEM((8, 4, 16, 128), BF),
            pltpu.VMEM((4, 8, 16, 128), BF),
            pltpu.VMEM((4, 8, 16, 512), BF),
            pltpu.VMEM((8, 4, 16, 512), BF),
            pltpu.VMEM((4, 8, 16, 512), BF),
        ]
        + [dma(shape) for shape in sems for _ in range(2)],
        compiler_params=pltpu.CompilerParams(
            collective_id=0, has_side_effects=True, vmem_limit_bytes=60 * 1024 * 1024
        ),
        cost_estimate=pl.CostEstimate(
            flops=6_000_000_000, bytes_accessed=8_000_000, transcendentals=500_000
        ),
    )(*operands)


def on_device(
    query_nope,
    query_rope,
    latent_cache,
    key_rope,
    lengths,
    key_weight,
    expert_input,
    route_slots,
    route_gates,
    trainer_gate_up,
    trainer_down,
    trainer_order,
    rollout_order,
):
    q_send = query_nope.reshape(4, NX, NY, 4, NOPE).transpose(2, 1, 0, 3, 4).reshape(8, 4, 16, 128)
    expert_output, latent_output = exchange(
        expert_input.reshape(4, 56, 128).transpose(1, 0, 2).reshape(224, 128),
        route_slots.T,
        route_gates.T,
        trainer_order,
        rollout_order,
        trainer_gate_up,
        trainer_down.reshape(256, 896),
        key_weight.reshape(32, 512),
        q_send,
        latent_cache,
        query_rope.transpose(0, 2, 1),
        key_rope.transpose(0, 2, 1),
        lengths,
    )
    return (latent_output, expert_output)


def solution(mesh):
    in_specs = (
        P(("dp", "expert"), None, None),
        P(("dp", "expert"), None, None),
        P(("dp", "expert"), None, None),
        P(("dp", "expert"), None, None),
        P(("dp", "expert")),
        P("expert", "dp", None),
        P(("dp", "expert"), None),
        P(("dp", "expert"), None),
        P(("dp", "expert"), None),
        P(None, "expert", None, "dp"),
        P(None, "expert", "dp"),
        P(),
        P(),
    )
    out_specs = (P(("dp", "expert"), None, None), P(("dp", "expert"), None))
    return jax.shard_map(
        on_device, mesh=mesh, in_specs=in_specs, out_specs=out_specs, check_vma=False
    )
```

time: 129 us -> 106 us (0.82)
  local copies, waits for them, and re-layouts: 16.1 us -> 4.94 us
  Pallas kernels: 105 us -> 99.8 us
  matrix products: 2.99 us -> 0 us
  other arithmetic: 2.27 us -> 0 us
    unnamed x35 -> x2, local copies, waits for them, and re-layouts: 9.62 us -> 3.33 us
    pallas_call x1, Pallas kernels: 105 us -> 99.8 us  [exchange(): pl.pallas_call(kernel, out_shape=(jax.ShapeDtypeStruct((4, 7168), BF), ja...]
    reshape x5 -> x0, local copies, waits for them, and re-layouts: 4.25 us -> none  [the longest x1 2.45 us: on_device(): trainer_gate_up.reshape(512, 896)]
    dot_general x3 -> x0, matrix products: 2.99 us -> none  [the longest x1 1.85 us: on_device(): jnp.einsum('rhl,rlk->rhk', attention, latent_cache, preferred_element_typ...]
    reshape x1, local copies, waits for them, and re-layouts: 0.05 us -> 1.61 us  [on_device(): query_nope.reshape(4, NX, NY, 4, NOPE).transpose(2, 1, 0, 3, 4)]
where the time goes in v2:
time: 106 us; the launch traced here: 105 us
  Pallas kernels  99.8 us (94%)
  local copies, waits for them, and re-layouts  4.94 us (5%)
    pallas_call x1, Pallas kernels, exchange(): pl.pallas_call(kernel, out_shape=(jax.ShapeDtypeStruct((4, 7168), BF), ja...  99.8 us
    unnamed x2, local copies, waits for them, and re-layouts  3.33 us

profile of v2, /device:TPU:6, one launch (start us, length us, event | category | flops | bytes accessed | tf_op | source)
XLA Modules:
  0.0 105.4 jit_solution(7532112208820813699)
XLA Ops:
  0.6 1.6 %copy.25 = bf16[4,4,8,4,128]{4,3,0,1,2:T(4,128)(2,1)} copy(bf16[4,4,8,4,128]{4,3,2,1,0:T(4,128)(2,1)} %bitcast.15) | data formatting | bytes 262144 | tf_op jit(solution)/shard_map/reshape | solution.py:565
  2.2 99.8 %shard_map.221 = (bf16[4,7168]{1,0:T(4,128)(2,1)}, bf16[4,128,512]{2,1,0:T(8,128)(2,1)}) custom-call(bf16[224,128]{1,0:T(8,128)(2,1)} %bitcast.20, s32[2,4]{1,0:T(2,128)} %bitcast.22, f32[2,4]{1,0:T(2,128)} %bitcast.23, s32[8]{0:T(128)} %trainer_hbm.1, s32[8]{0:T(128)} %rollout_hbm.1, bf16[8,32,2,896]{3,2,1,0:T(2,128)(2,1)} %w_raw_hbm.1, ...), custom_call_target="tpu_custom_call" | custom-call | flops 6000000000 | bytes 8000000 | tf_op jit(solution)/shard_map/pallas_call | solution.py:506
  102.1 1.9 %copy.28 = bf16[4,128,512]{2,1,0:T(8,128)(2,1)} copy(bf16[4,128,512]{2,1,0:T(8,128)(2,1)} %get-tuple-element.8) | data formatting | bytes 1048576
  104.0 1.5 %copy.29 = bf16[4,7168]{1,0:T(4,128)(2,1)} copy(bf16[4,7168]{1,0:T(4,128)(2,1)} %get-tuple-element.9) | data formatting | bytes 114688

commit v3 on v2

--- a/solution.py
+++ b/solution.py
@@ -16,6 +16,8 @@
 MESH = pl.DeviceIdType.MESH
 SCORE_SCALE = 1.0 / math.sqrt(NOPE + ROPE)
 X_ORDER = (0, 1, 3, 2)
+NEAR_FIRST = (1, 7, 2, 6, 3, 5, 4)
+FAR_FIRST = (4, 3, 5, 2, 6, 1, 7)
 FORWARD_PLUS = (0, 2, 5, 7)
 FORWARD_MINUS = (1, 3, 4, 6)
 
@@ -67,14 +69,14 @@
     perm_hbm, perm_t_hbm, mask_in_hbm, pick_hbm, gate_hbm, spread_hbm, mask_out_hbm, repeat_hbm,
     by_row_hbm,
     out_rows, out_latent,
-    x_in, slots, gates, trainer, rollout, w_raw, w_out, key_own, q_send,
+    x_in, slots, gates, trainer, rollout, w_raw, w_out, key_own, q_in,
     cache, q_rope, k_rope, lengths,
     perm, perm_t, mask_in, pick, gate, spread, mask_out, repeat, by_row,
-    pieces, w_in, lat_rows, s_load,
-    got, rows, part, part_got, hid, share, share_sib, ring_out, ring_in, col_sum, col_got,
+    pieces, w_in, lat_rows, q_send, s_load,
+    got, rows, part, part_got, hid, share, share_sib, ring_out, ring_in,
     back_out, back_got, keys, q_col, q_own, lat_own, lat_col, lat_got,
     s_piece, r_piece, s_ring, r_ring, s_x, r_x, s_fwd, r_fwd, s_sib, r_sib,
-    s_part, r_part, s_hid, r_hid, s_ssib, r_ssib, s_red, r_red, s_col, r_col, s_back, r_back,
+    s_part, r_part, s_hid, r_hid, s_ssib, r_ssib, s_red, r_red, s_back, r_back,
     s_key, r_key, s_ksib, r_ksib, s_qy, r_qy, s_qx, r_qx, s_ly, r_ly, s_lx, r_lx,
 ):
     z = lax.axis_index("dp")
@@ -99,6 +101,9 @@
     def on_x(d):
         return (z, (at_x(d) * NY + y) * 2 + c)
 
+    def on_xz(dx, dz):
+        return (at_z(dz), (at_x(dx) * NY + y) * 2 + c)
+
     def on_y(d):
         return (z, (x * NY + at_y(d)) * 2 + c)
 
@@ -110,7 +115,7 @@
             (
                 (x_hbm, x_in), (slots_hbm, slots), (gates_hbm, gates),
                 (trainer_hbm, trainer), (rollout_hbm, rollout),
-                (key_hbm, key_own), (q_hbm, q_send), (perm_hbm, perm),
+                (key_hbm, key_own), (q_hbm, q_in), (perm_hbm, perm),
                 (w_raw_hbm, w_raw), (repeat_hbm, repeat),
                 (mask_in_hbm, mask_in), (pick_hbm, pick), (gate_hbm, gate),
                 (spread_hbm, spread), (mask_out_hbm, mask_out), (w_out_hbm, w_out),
@@ -125,7 +130,7 @@
 
     barrier = pltpu.get_barrier_semaphore()
     peers = [on_z(d) for d in range(1, NZ)] + [on_y(d) for d in range(1, NY)]
-    peers += [on_x(d) for d in range(1, NX)] + [sibling]
+    peers += [on_xz(dx, dz) for dx in range(1, NX) for dz in range(NZ)] + [sibling]
     for peer in peers:
         pl.semaphore_signal(barrier, inc=1, device_id=peer, device_id_type=MESH)
 
@@ -168,15 +173,20 @@
 
     piece = [
         send(pieces.at[at_z(d)], got.at[z], s_piece.at[d - 1], r_piece.at[d - 1], on_z(d))
-        for d in range(1, NZ)
+        for d in FAR_FIRST
     ]
     loads[6].wait()
+    loads[17].wait()
+    turned = lax.dot_general(
+        by_row[...], q_in[...], (((0,), (0,)), ((), ())), preferred_element_type=F32
+    )
+    q_send[...] = turned.astype(BF).reshape(4, 8, 16, 128)
     q_y = [
-        send(q_send.at[at_y(d)], q_col.at[y], s_qy.at[d - 1], r_qy.at[d - 1], on_y(d))
-        for d in range(1, NY)
+        send(q_send.at[:, at_y(d)], q_col.at[y], s_qy.at[d - 1], r_qy.at[d - 1], on_y(d))
+        for d in FAR_FIRST
     ]
     got[z] = pieces[z]
-    q_col[y] = q_send[y]
+    q_col[y] = q_send[:, y]
     loads[5].wait()
     keys[c, z] = key_own[...]
 
@@ -209,16 +219,15 @@
             b = block(at_x(3), origins[k])
             far.append(send(b, b, s_fwd.at[k], r_fwd.at[k], on_x(1)))
 
-    def ring(origin, way, step):
-        b = block(x, origin)
-        peer = on_y(sign) if way == 0 else on_y(-sign)
-        return send(b, b, s_ring.at[way, step], r_ring.at[way, step], peer)
-
-    plus, minus = ring(y, 0, 0), ring(y, 1, 0)
+    own = block(x, y)
+    y_copies = [
+        send(own, own, s_ring.at[i], r_ring.at[i], on_y(sign * d))
+        for i, d in enumerate((1, -1, 2, -2))
+    ]
     to_x(y)
     key_z = [
         send(key_own, keys.at[c, z], s_key.at[d - 1], r_key.at[d - 1], on_z(d))
-        for d in range(1, NZ)
+        for d in FAR_FIRST
     ]
     for copy in q_y:
         copy.wait_recv()
@@ -227,34 +236,31 @@
         for d in range(1, NX)
     ]
     q_own[x] = q_col[:, x]
-    for step in range(1, 5):
-        plus.wait_recv()
-        origin = at_y(-sign * step)
-        if step < 4:
-            plus = ring(origin, 0, step)
-        to_x(origin)
-        if step < 4:
-            minus.wait_recv()
-            origin = at_y(sign * step)
-            if step < 3:
-                minus = ring(origin, 1, step)
-            to_x(origin)
+    loads[8].wait()
+
+    def line_up(i, carry):
+        start = pl.multiple_of(i * 64, 64)
+        w_in[pl.ds(start, 64), :] = w_raw[i].reshape(64, 896)
+        return carry
+
+    for step, d in enumerate((-1, 1, -2, 2, -3, 3, -4)):
+        y_copies[step].wait_recv()
+        b = block(x, at_y(sign * d))
+        if d == -2:
+            y_copies.append(send(b, b, s_ring.at[4], r_ring.at[4], on_y(sign)))
+            far_y = send(b, b, s_ring.at[6], r_ring.at[6], on_y(2 * sign))
+        if d == 2:
+            y_copies.append(send(b, b, s_ring.at[5], r_ring.at[5], on_y(-sign)))
+            y_copies.append(far_y)
+        to_x(at_y(sign * d))
         if step == 1:
-            loads[8].wait()
-
-            def line_up(i, carry):
-                start = pl.multiple_of(i * 64, 64)
-                w_in[pl.ds(start, 64), :] = w_raw[i].reshape(64, 896)
-                return carry
-
             lax.fori_loop(0, 8, line_up, 0)
-        if step == 2:
-            for load in loads[9:]:
+        if step == 3:
+            for load in loads[9:17] + loads[18:]:
                 load.wait()
-            pass_on(0)
-        if step == 3:
-            pass_on(1)
-            pass_on(2)
+        if step == 5:
+            for k in range(3):
+                pass_on(k)
             for copy in key_z:
                 copy.wait_recv()
             key_sib = send(keys.at[c], keys.at[c], s_ksib.at[0], r_ksib.at[0], sibling)
@@ -285,7 +291,7 @@
                 part.at[at_z(d), js], part_got.at[d - 1, js],
                 s_part.at[group[0], d - 1], r_part.at[group[0], d - 1], on_z(d),
             )
-            for d in range(1, NZ)
+            for d in FAR_FIRST
         ]
 
     def activate(group, arriving):
@@ -308,7 +314,7 @@
                 hid.at[z, js], hid.at[z, js],
                 s_hid.at[group[0], d - 1], r_hid.at[group[0], d - 1], on_z(d),
             )
-            for d in range(1, NZ)
+            for d in FAR_FIRST
         ]
 
     def project_down(group, arriving):
@@ -335,43 +341,72 @@
     def own_share(j, target):
         return share[j, c, target].astype(F32) + share_sib[j, target].astype(F32)
 
-    def reduce_step(group, step, state):
-        new = [None, None]
+    def move_sum(group, i, offset, to, arrived):
+        js = pl.ds(group[0], len(group))
+        target = at_y(sign * offset)
+        for j in group:
+            value = own_share(j, target)
+            for k in arrived:
+                value = value + ring_in[k, j].astype(F32)
+            ring_out[i, j] = value.astype(BF)
+        return send(
+            ring_out.at[i, js], ring_in.at[i, js],
+            s_red.at[group[0], i], r_red.at[group[0], i], on_y(sign * to),
+        )
+
+    def reduce_first(group, arriving):
+        for copy in arriving:
+            copy.wait_recv()
+        hops = ((4, 3), (3, 2), (-3, -2), (2, 1), (-2, -1))
+        return [move_sum(group, i, offset, to, ()) for i, (offset, to) in enumerate(hops)]
+
+    def reduce_second(group, arriving):
+        for i in (4, 2):
+            arriving[i].wait_recv()
+        copies = [move_sum(group, 6, -1, -1, (2, 4))]
+        for i in (3, 1, 0):
+            arriving[i].wait_recv()
+        return copies + [move_sum(group, 5, 1, 1, (0, 1, 3))]
+
+    def ring_step(group, step, state):
         if step == 1:
             for copy in state:
                 copy.wait_recv()
-        js = pl.ds(group[0], len(group))
+        new = [None, None]
         for way, hops in ((0, 4), (1, 3)):
             if step > hops:
                 new[way] = state[way]
                 continue
-            target = at_y(sign * (hops + 1 - step) * (1 - 2 * way))
+            arrived = ()
             if step > 1:
                 state[way].wait_recv()
-            for j in group:
-                value = own_share(j, target)
-                if step > 1:
-                    value = value + ring_in[way, step - 2, j].astype(F32)
-                ring_out[way, step - 1, j] = value.astype(BF)
-            new[way] = send(
-                ring_out.at[way, step - 1, js], ring_in.at[way, step - 1, js],
-                s_red.at[group[0], way, step - 1], r_red.at[group[0], way, step - 1],
-                on_y(sign * (1 - 2 * way)),
+                arrived = (way * 4 + step - 2,)
+            toward = 1 - 2 * way
+            new[way] = move_sum(
+                group, way * 4 + step - 1, toward * (hops + 1 - step), toward, arrived
             )
         return new
 
-    def reduce_end(group, state):
-        state[0].wait_recv()
-        state[1].wait_recv()
+    def reduce_end(group, arriving, last=(5, 6)):
+        for copy in arriving:
+            copy.wait_recv()
         copies = []
         for j in group:
-            value = own_share(j, y) + ring_in[0, 3, j].astype(F32) + ring_in[1, 2, j].astype(F32)
-            col_sum[j] = value.astype(BF)
-            if j > 0:
+            value = own_share(j, y)
+            for k in last:
+                value = value + ring_in[k, j].astype(F32)
+            value = value.astype(BF)
+            tiles = [value[:, t * 128 : (t + 1) * 128] for t in range(7)]
+            tiles = jnp.concatenate(tiles + [jnp.zeros((32, 128), BF)], axis=0)
+            back_out[j] = dot(perm_t[...], tiles).astype(BF).reshape(8, 32, 128)
+            for d in FAR_FIRST + (0,):
+                if j == 0 and d == 0:
+                    back_got[j, z] = back_out[j, z]
+                    continue
                 copies.append(
                     send(
-                        col_sum.at[j], col_got.at[j - 1],
-                        s_col.at[j - 1], r_col.at[j - 1], on_x(X_ORDER[j]),
+                        back_out.at[j, at_z(d)], back_got.at[j, z],
+                        s_back.at[j, d], r_back.at[j, d], on_xz(X_ORDER[j], d),
                     )
                 )
         return copies
@@ -388,7 +423,7 @@
         lat_own[...] = dot(wide, keys[...].reshape(512, 512)).astype(BF).reshape(4, 8, 16, 512)
         copies = [
             send(lat_own.at[:, at_y(d)], lat_col.at[y], s_ly.at[d - 1], r_ly.at[d - 1], on_y(d))
-            for d in range(1, NY)
+            for d in FAR_FIRST
         ]
         lat_col[y] = lat_own[:, y]
         return copies
@@ -423,9 +458,9 @@
 
     one, two, three = (0,), (1, 2), (3,)
     sib = [to_sibling(0)]
-    lat_y = absorb()
     sib[0].wait_recv()
     part_1 = project(one)
+    lat_y = absorb()
     for k in range(3, 8):
         pass_on(k)
     sib.append(to_sibling(1))
@@ -433,59 +468,48 @@
     sib[1].wait_recv()
     sib[2].wait_recv()
     part_2 = project(two)
-    hid_1 = activate(one, part_1)
     for copy in far:
         copy.wait_recv()
     sib.append(to_sibling(3))
+    hid_1 = activate(one, part_1)
     sib[3].wait_recv()
     part_3 = project(three)
-    down_1 = project_down(one, hid_1)
+    sums_1 = project_down(one, hid_1)
     hid_2 = activate(two, part_2)
+    sums_1 = ring_step(one, 1, sums_1)
+    hid_3 = activate(three, part_3)
+    sums_1 = ring_step(one, 2, sums_1)
     lat_x = latent_x(lat_y)
-    red_1 = reduce_step(one, 1, down_1)
-    hid_3 = activate(three, part_3)
-    down_2 = project_down(two, hid_2)
-    red_1 = reduce_step(one, 2, red_1)
-    down_3 = project_down(three, hid_3)
-    red_2 = reduce_step(two, 1, down_2)
-    red_1 = reduce_step(one, 3, red_1)
-    red_3 = reduce_step(three, 1, down_3)
-    red_1 = reduce_step(one, 4, red_1)
+    sums_2 = project_down(two, hid_2)
+    sums_1 = ring_step(one, 3, sums_1)
+    sums_3 = project_down(three, hid_3)
+    sums_2 = ring_step(two, 1, sums_2)
+    sums_3 = ring_step(three, 1, sums_3)
+    sums_1 = ring_step(one, 4, sums_1)
     latent_end(lat_x)
-    red_2 = reduce_step(two, 2, red_2)
-    red_3 = reduce_step(three, 2, red_3)
+    sums_2 = ring_step(two, 2, sums_2)
+    sums_3 = ring_step(three, 2, sums_3)
     attend(0)
-    red_2 = reduce_step(two, 3, red_2)
-    red_3 = reduce_step(three, 3, red_3)
-    reduce_end(one, red_1)
+    sums_2 = ring_step(two, 3, sums_2)
+    sums_3 = ring_step(three, 3, sums_3)
+    backs = reduce_end(one, sums_1, (3, 6))
     attend(1)
-    red_2 = reduce_step(two, 4, red_2)
-    red_3 = reduce_step(three, 4, red_3)
+    sums_2 = ring_step(two, 4, sums_2)
+    sums_3 = ring_step(three, 4, sums_3)
     attend(2)
-    cols = reduce_end(two, red_2)
-    cols += reduce_end(three, red_3)
+    backs += reduce_end(two, sums_2, (3, 6))
+    backs += reduce_end(three, sums_3, (3, 6))
     attend(3)
 
-    total = col_sum[0].astype(F32)
-    for j in range(3):
-        cols[j].wait_recv()
-        total = total + col_got[j].astype(F32)
-    total = total.astype(BF)
-    tiles = [total[:, t * 128 : (t + 1) * 128] for t in range(7)] + [jnp.zeros((32, 128), BF)]
-    tiles = jnp.concatenate(tiles, axis=0)
-    back_out[...] = dot(perm_t[...], tiles).astype(BF).reshape(8, 32, 128)
-    back = [
-        send(back_out.at[at_z(d)], back_got.at[z], s_back.at[d - 1], r_back.at[d - 1], on_z(d))
-        for d in range(1, NZ)
-    ]
-    back_got[z] = back_out[z]
-    for copy in back:
+    for copy in backs:
         copy.wait_recv()
     for d in range(NZ):
-        part_rows = back_got[d].astype(F32)
+        total = back_got[0, d].astype(F32)
+        for j in range(1, NX):
+            total = total + back_got[j, d].astype(F32)
         for t in range(7):
             first = (d * 7 + t) * 128
-            out_rows[:, first : first + 128] = part_rows[t * 4 : t * 4 + 4].astype(BF)
+            out_rows[:, first : first + 128] = total[t * 4 : t * 4 + 4].astype(BF)
     for copy in sent:
         copy.wait_send()
 
@@ -493,8 +517,8 @@
 def exchange(*operands):
     dma = pltpu.SemaphoreType.DMA
     sems = [
-        (7,), (2, 4), (2, 8), (8,), (4,),
-        (4, 7), (4, 7), (4,), (4, 2, 4), (3,), (7,),
+        (7,), (7,), (2, 8), (8,), (4,),
+        (4, 7), (4, 7), (4,), (4, 7), (4, 8),
         (7,), (1,), (7,), (3,), (7,), (3,),
     ]
     vmem = pl.BlockSpec(memory_space=pltpu.VMEM)
@@ -516,6 +540,7 @@
             pltpu.VMEM((8, 32, 128), BF),
             pltpu.VMEM((512, 896), BF),
             pltpu.VMEM((4, 128, 512), BF),
+            pltpu.VMEM((4, 8, 16, 128), BF),
             dma((len(operands),)),
             pltpu.VMEM((8, 32, 128), BF),
             pltpu.VMEM((4, 2, 8, 32, 1024), BF),
@@ -524,12 +549,10 @@
             pltpu.VMEM((8, 4, 32, 128), BF),
             pltpu.VMEM((4, 2, 8, 32, 896), BF),
             pltpu.VMEM((4, 8, 32, 896), BF),
-            pltpu.VMEM((2, 4, 4, 32, 896), BF),
-            pltpu.VMEM((2, 4, 4, 32, 896), BF),
-            pltpu.VMEM((4, 32, 896), BF),
-            pltpu.VMEM((3, 32, 896), BF),
-            pltpu.VMEM((8, 32, 128), BF),
-            pltpu.VMEM((8, 32, 128), BF),
+            pltpu.VMEM((7, 4, 32, 896), BF),
+            pltpu.VMEM((7, 4, 32, 896), BF),
+            pltpu.VMEM((4, 8, 32, 128), BF),
+            pltpu.VMEM((4, 8, 32, 128), BF),
             pltpu.VMEM((2, 8, 32, 512), BF),
             pltpu.VMEM((8, 4, 16, 128), BF),
             pltpu.VMEM((4, 8, 16, 128), BF),
@@ -547,6 +570,20 @@
     )(*operands)
 
 
+def place(rows, latent):
+    def body(rows_in, latent_in, rows_out, latent_out):
+        rows_out[...] = rows_in[...]
+        latent_out[...] = latent_in[...]
+
+    vmem = pl.BlockSpec(memory_space=pltpu.VMEM)
+    return pl.pallas_call(
+        body,
+        out_shape=tuple(jax.ShapeDtypeStruct(a.shape, a.dtype) for a in (rows, latent)),
+        in_specs=[vmem, vmem],
+        out_specs=(vmem, vmem),
+    )(rows, latent)
+
+
 def on_device(
     query_nope,
     query_rope,
@@ -562,7 +599,6 @@
     trainer_order,
     rollout_order,
 ):
-    q_send = query_nope.reshape(4, NX, NY, 4, NOPE).transpose(2, 1, 0, 3, 4).reshape(8, 4, 16, 128)
     expert_output, latent_output = exchange(
         expert_input.reshape(4, 56, 128).transpose(1, 0, 2).reshape(224, 128),
         route_slots.T,
@@ -572,12 +608,13 @@
         trainer_gate_up,
         trainer_down.reshape(256, 896),
         key_weight.reshape(32, 512),
-        q_send,
+        query_nope.reshape(512, 128),
         latent_cache,
         query_rope.transpose(0, 2, 1),
         key_rope.transpose(0, 2, 1),
         lengths,
     )
+    expert_output, latent_output = place(expert_output, latent_output)
     return (latent_output, expert_output)
 
 

time: 106 us -> 96 us (0.906)
  local copies, waits for them, and re-layouts: 4.94 us -> 0 us
  Pallas kernels: 99.8 us -> 95 us
    pallas_call x1, Pallas kernels: 99.8 us -> 93.1 us  [exchange(): pl.pallas_call(kernel, out_shape=(jax.ShapeDtypeStruct((4, 7168), BF), ja...]
    unnamed x2 -> x0, local copies, waits for them, and re-layouts: 3.33 us -> none
    pallas_call x0 -> x1, Pallas kernels: none -> 1.91 us  [place(): pl.pallas_call(body, out_shape=tuple((jax.ShapeDtypeStruct(a.shape, a.dty...]
    reshape x1 -> x0, local copies, waits for them, and re-layouts: 1.61 us -> none  [on_device(): query_nope.reshape(4, NX, NY, 4, NOPE).transpose(2, 1, 0, 3, 4)]
where the time goes in v3:
time: 96 us; the launch traced here: 95.6 us
  Pallas kernels  95 us (99%)
    pallas_call x1, Pallas kernels, exchange(): pl.pallas_call(kernel, out_shape=(jax.ShapeDtypeStruct((4, 7168), BF), ja...  93.1 us

profile of v3, /device:TPU:6, one launch (start us, length us, event | category | flops | bytes accessed | tf_op | source)
XLA Modules:
  0.0 95.6 jit_solution(11824249874157118879)
XLA Ops:
  0.6 93.1 %shard_map.221 = (bf16[4,7168]{1,0:T(4,128)(2,1)}, bf16[4,128,512]{2,1,0:T(8,128)(2,1)}) custom-call(bf16[224,128]{1,0:T(8,128)(2,1)} %bitcast.16, s32[2,4]{1,0:T(2,128)} %bitcast.18, f32[2,4]{1,0:T(2,128)} %bitcast.19, s32[8]{0:T(128)} %trainer_hbm.1, s32[8]{0:T(128)} %rollout_hbm.1, bf16[8,32,2,896]{3,2,1,0:T(2,128)(2,1)} %w_raw_hbm.1, ...), custom_call_target="tpu_custom_call" | custom-call | flops 6000000000 | bytes 8000000 | tf_op jit(solution)/shard_map/pallas_call | solution.py:530
  93.7 1.9 %shard_map.222 = (bf16[4,7168]{1,0:T(4,128)(2,1)}, bf16[4,128,512]{2,1,0:T(8,128)(2,1)}) custom-call(bf16[4,7168]{1,0:T(4,128)(2,1)} %get-tuple-element.6.rows_in, bf16[4,128,512]{2,1,0:T(8,128)(2,1)} %get-tuple-element.7.latent_in), custom_call_target="tpu_custom_call" | custom-call | tf_op jit(solution)/shard_map/pallas_call | solution.py:579

commit v4 on v3

--- a/solution.py
+++ b/solution.py
@@ -465,34 +465,34 @@
         pass_on(k)
     sib.append(to_sibling(1))
     sib.append(to_sibling(2))
+    hid_1 = activate(one, part_1)
     sib[1].wait_recv()
     sib[2].wait_recv()
     part_2 = project(two)
     for copy in far:
         copy.wait_recv()
     sib.append(to_sibling(3))
-    hid_1 = activate(one, part_1)
+    sums_1 = project_down(one, hid_1)
     sib[3].wait_recv()
     part_3 = project(three)
-    sums_1 = project_down(one, hid_1)
+    sums_1 = ring_step(one, 1, sums_1)
     hid_2 = activate(two, part_2)
-    sums_1 = ring_step(one, 1, sums_1)
+    lat_x = latent_x(lat_y)
+    sums_1 = ring_step(one, 2, sums_1)
     hid_3 = activate(three, part_3)
-    sums_1 = ring_step(one, 2, sums_1)
-    lat_x = latent_x(lat_y)
+    sums_1 = ring_step(one, 3, sums_1)
     sums_2 = project_down(two, hid_2)
-    sums_1 = ring_step(one, 3, sums_1)
+    sums_1 = ring_step(one, 4, sums_1)
     sums_3 = project_down(three, hid_3)
     sums_2 = ring_step(two, 1, sums_2)
     sums_3 = ring_step(three, 1, sums_3)
-    sums_1 = ring_step(one, 4, sums_1)
+    backs = reduce_end(one, sums_1, (3, 6))
     latent_end(lat_x)
     sums_2 = ring_step(two, 2, sums_2)
     sums_3 = ring_step(three, 2, sums_3)
     attend(0)
     sums_2 = ring_step(two, 3, sums_2)
     sums_3 = ring_step(three, 3, sums_3)
-    backs = reduce_end(one, sums_1, (3, 6))
     attend(1)
     sums_2 = ring_step(two, 4, sums_2)
     sums_3 = ring_step(three, 4, sums_3)

time: 96 us -> 92.3 us (0.961)
  Pallas kernels: 95 us -> 91.6 us
    pallas_call x1, Pallas kernels: 93.1 us -> 89.6 us  [exchange(): pl.pallas_call(kernel, out_shape=(jax.ShapeDtypeStruct((4, 7168), BF), ja...]
where the time goes in v4:
time: 92.3 us; the launch traced here: 92.2 us
  Pallas kernels  91.6 us (99%)
    pallas_call x1, Pallas kernels, exchange(): pl.pallas_call(kernel, out_shape=(jax.ShapeDtypeStruct((4, 7168), BF), ja...  89.6 us
    pallas_call x1, Pallas kernels, place(): pl.pallas_call(body, out_shape=tuple((jax.ShapeDtypeStruct(a.shape, a.dty...  1.91 us

profile of v4, /device:TPU:6, one launch (start us, length us, event | category | flops | bytes accessed | tf_op | source)
XLA Modules:
  0.0 92.2 jit_solution(10266391018981598993)
XLA Ops:
  0.6 89.6 %shard_map.221 = (bf16[4,7168]{1,0:T(4,128)(2,1)}, bf16[4,128,512]{2,1,0:T(8,128)(2,1)}) custom-call(bf16[224,128]{1,0:T(8,128)(2,1)} %bitcast.16, s32[2,4]{1,0:T(2,128)} %bitcast.18, f32[2,4]{1,0:T(2,128)} %bitcast.19, s32[8]{0:T(128)} %trainer_hbm.1, s32[8]{0:T(128)} %rollout_hbm.1, bf16[8,32,2,896]{3,2,1,0:T(2,128)(2,1)} %w_raw_hbm.1, ...), custom_call_target="tpu_custom_call" | custom-call | flops 6000000000 | bytes 8000000 | tf_op jit(solution)/shard_map/pallas_call | solution.py:530
  90.3 1.9 %shard_map.222 = (bf16[4,7168]{1,0:T(4,128)(2,1)}, bf16[4,128,512]{2,1,0:T(8,128)(2,1)}) custom-call(bf16[4,7168]{1,0:T(4,128)(2,1)} %get-tuple-element.6.rows_in, bf16[4,128,512]{2,1,0:T(8,128)(2,1)} %get-tuple-element.7.latent_in), custom_call_target="tpu_custom_call" | custom-call | tf_op jit(solution)/shard_map/pallas_call | solution.py:579

commit v5 on v4

--- a/solution.py
+++ b/solution.py
@@ -460,11 +460,11 @@
     sib = [to_sibling(0)]
     sib[0].wait_recv()
     part_1 = project(one)
-    lat_y = absorb()
     for k in range(3, 8):
         pass_on(k)
     sib.append(to_sibling(1))
     sib.append(to_sibling(2))
+    lat_y = absorb()
     hid_1 = activate(one, part_1)
     sib[1].wait_recv()
     sib[2].wait_recv()

time: 92.3 us -> 93 us (level)
  no operation moved by 1% of the time
where the time goes in v5:
time: 93 us; the launch traced here: 92.5 us
  Pallas kernels  91.9 us (99%)
    pallas_call x1, Pallas kernels, exchange(): pl.pallas_call(kernel, out_shape=(jax.ShapeDtypeStruct((4, 7168), BF), ja...  90 us
    pallas_call x1, Pallas kernels, place(): pl.pallas_call(body, out_shape=tuple((jax.ShapeDtypeStruct(a.shape, a.dty...  1.91 us

profile of v5, /device:TPU:6, one launch (start us, length us, event | category | flops | bytes accessed | tf_op | source)
XLA Modules:
  0.0 92.5 jit_solution(10116622838306615659)
XLA Ops:
  0.6 90.0 %shard_map.221 = (bf16[4,7168]{1,0:T(4,128)(2,1)}, bf16[4,128,512]{2,1,0:T(8,128)(2,1)}) custom-call(bf16[224,128]{1,0:T(8,128)(2,1)} %bitcast.16, s32[2,4]{1,0:T(2,128)} %bitcast.18, f32[2,4]{1,0:T(2,128)} %bitcast.19, s32[8]{0:T(128)} %trainer_hbm.1, s32[8]{0:T(128)} %rollout_hbm.1, bf16[8,32,2,896]{3,2,1,0:T(2,128)(2,1)} %w_raw_hbm.1, ...), custom_call_target="tpu_custom_call" | custom-call | flops 6000000000 | bytes 8000000 | tf_op jit(solution)/shard_map/pallas_call | solution.py:530
  90.6 1.9 %shard_map.222 = (bf16[4,7168]{1,0:T(4,128)(2,1)}, bf16[4,128,512]{2,1,0:T(8,128)(2,1)}) custom-call(bf16[4,7168]{1,0:T(4,128)(2,1)} %get-tuple-element.6.rows_in, bf16[4,128,512]{2,1,0:T(8,128)(2,1)} %get-tuple-element.7.latent_in), custom_call_target="tpu_custom_call" | custom-call | tf_op jit(solution)/shard_map/pallas_call | solution.py:579
